TPU v7x, 32 devices: a whole 2x2x4 slice. The times are simulated.
32 devices in a mesh: dp: 4 (over z), emb: 8 (over y, x, core).
Axes of the slice: x: 2, y: 2, z: 4, core: 2. Of those that a mesh axis runs over, the one named last changes fastest.
Arguments:
- pixels: bfloat16 [32768, 768], P(('dp', 'emb')), may hold values from -6 to 6
- counts: int32 [32, 2], P(('dp', 'emb')), may hold values from 0 to 511, as said below
- token_ids: int32 [32768], P(('dp', 'emb')), may hold values from 0 to 31999, as said below
- action_bins: int32 [32768], P(('dp', 'emb')), may hold values from 0 to 1023
- patch_pos: int32 [32768], P(('dp', 'emb')), may hold values from 0 to 255
- token_table: bfloat16 [33024, 768], P('emb'), may hold values from -6 to 6
- pos_table: bfloat16 [256, 768], replicated, may hold values from -4 to 4
- w_patch: bfloat16 [768, 768], replicated, may hold values from -0.21875 to 0.21875
- w_res_a: bfloat16 [768, 768], replicated, may hold values from -0.21875 to 0.21875
- w_res_b: bfloat16 [768, 768], replicated, may hold values from -0.21875 to 0.21875
- gain_one: bfloat16 [768], replicated, may hold values from 0.5 to 1.5
- bias_one: bfloat16 [768], replicated, may hold values from -2 to 2
- w_q: bfloat16 [768, 768], replicated, may hold values from -0.21875 to 0.21875
- w_k: bfloat16 [768, 768], replicated, may hold values from -0.21875 to 0.21875
- w_v: bfloat16 [768, 768], replicated, may hold values from -0.21875 to 0.21875
- w_o: bfloat16 [768, 768], replicated, may hold values from -1 to 1
- gain_two: bfloat16 [768], replicated, may hold values from 0.5 to 1.5
- bias_two: bfloat16 [768], replicated, may hold values from -2 to 2
- w_up: bfloat16 [768, 3072], replicated, may hold values from -0.21875 to 0.21875
- w_down: bfloat16 [3072, 768], replicated, may hold values from -0.109375 to 0.109375
- cotangent: bfloat16 [32768, 768], P(('dp', 'emb')), may hold values from -6 to 6
Outputs:
- output: bfloat16 [32768, 768], P(('dp', 'emb'))
- grad_pixels: float32 [32768, 768], P(('dp', 'emb'))
- grad_table: float32 [33024, 768], P('emb', 'dp')
- grad_pos_table: float32 [256, 768], P(('dp', 'emb'))
- grad_w_patch: float32 [768, 768], P(('dp', 'emb'))
- grad_w_res_a: float32 [768, 768], P(('dp', 'emb'))
- grad_w_res_b: float32 [768, 768], P(('dp', 'emb'))
- grad_gain_one: float32 [768], P(('dp', 'emb'))
- grad_bias_one: float32 [768], P(('dp', 'emb'))
- grad_w_q: float32 [768, 768], P(('dp', 'emb'))
- grad_w_k: float32 [768, 768], P(('dp', 'emb'))
- grad_w_v: float32 [768, 768], P(('dp', 'emb'))
- grad_w_o: float32 [768, 768], P(('dp', 'emb'))
- grad_gain_two: float32 [768], P(('dp', 'emb'))
- grad_bias_two: float32 [768], P(('dp', 'emb'))
- grad_w_up: float32 [768, 3072], P(('dp', 'emb'))
- grad_w_down: float32 [3072, 768], P(('dp', 'emb'))
Inputs may be any that keep to these rules, and one draw needn't show every extreme that they name: Sequence s opens with counts[s, 0] image patches and closes with counts[s, 1] actions, 1 to 192 of them; text fills the rest. Some sequence has no patches, some has 511, some has 192 actions. `token_ids`: text ids are under 32000. Of one sequence's text and action tokens (an action's row is 32000 + its bin), at most 192 have rows in one aligned block of 4128 table rows, and in each sequence some block has exactly 192.
All inputs are finite; a program needn't handle non-finite values.
Results may differ from a plain program's by a relative error of at most 0.02.
Values may be sent and summed in bfloat16 or wider, within the bound.
A program may use at most 576 MiB of HBM per device.

v0:
```python
import jax
import jax.numpy as jnp
from jax import lax
from jax.sharding import PartitionSpec as P

HEAD_DIM = 32
TEXT_VOCAB = 32000


exact_precision = lax.Precision.HIGHEST


def normalize(values):
    average = jnp.mean(values, -1, keepdims=True)
    centred = values - average
    variance = jnp.mean(centred * centred, -1, keepdims=True)
    return centred * lax.rsqrt(variance + 1e-05)


def norm_affine(values, gain, offset):
    return normalize(values) * gain + offset


def product(left, right):
    return jnp.dot(left, right, preferred_element_type=jnp.float32)


def product_left(left, right):
    return lax.dot_general(
        left, right, (((0,), (0,)), ((), ())), preferred_element_type=jnp.float32
    )


def product_right(left, right):
    return lax.dot_general(
        left, right, (((1,), (1,)), ((), ())), preferred_element_type=jnp.float32
    )


def score_block(query_block, key_heads, block_start):
    scores = jnp.einsum(
        "qhd,khd->hqk", query_block, key_heads, preferred_element_type=jnp.float32
    ) * HEAD_DIM ** (-0.5)
    query_place = block_start + jnp.arange(query_block.shape[0])
    key_place = jnp.arange(key_heads.shape[0])
    allowed = key_place[None, :] <= query_place[:, None]
    return jnp.where(allowed[None], scores, -1e30)


def attention_forward(queries, key_heads, value_heads):
    length = queries.shape[0]
    head_count = queries.shape[1]
    block_rows = min(512, length)
    group_heads = min(12, head_count)
    pieces = []
    log_totals = []
    for block_start in range(0, length, block_rows):
        parts = []
        block_logs = []
        for head_start in range(0, head_count, group_heads):
            head_end = head_start + group_heads
            scores = score_block(
                queries[block_start : block_start + block_rows, head_start:head_end],
                key_heads[:, head_start:head_end],
                block_start,
            )
            highest = jnp.max(scores, -1, keepdims=True)
            weights = jnp.exp(scores - highest)
            totals = jnp.sum(weights, -1, keepdims=True)
            softmax_low = (weights / totals).astype(jnp.bfloat16)
            parts.append(
                jnp.einsum(
                    "hqk,khd->qhd",
                    softmax_low,
                    value_heads[:, head_start:head_end],
                    preferred_element_type=jnp.float32,
                )
            )
            block_logs.append(highest + jnp.log(totals))
        pieces.append(jnp.concatenate(parts, 1))
        log_totals.append(block_logs)
    return (jnp.concatenate(pieces, 0), log_totals)


def attention_backward(queries, key_heads, value_heads, grad_attended, log_totals):
    length = queries.shape[0]
    head_count = queries.shape[1]
    block_rows = min(512, length)
    group_heads = min(12, head_count)
    group_count = head_count // group_heads
    scaling = HEAD_DIM ** (-0.5)
    grad_queries = []
    key_sums = [
        jnp.zeros((length, group_heads, HEAD_DIM), jnp.float32) for group in range(group_count)
    ]
    value_sums = [
        jnp.zeros((length, group_heads, HEAD_DIM), jnp.float32) for group in range(group_count)
    ]
    for number, block_start in enumerate(range(0, length, block_rows)):
        query_parts = []
        for group in range(group_count):
            head_start = group * group_heads
            head_end = head_start + group_heads
            query_block = queries[block_start : block_start + block_rows, head_start:head_end]
            grad_block = grad_attended[block_start : block_start + block_rows, head_start:head_end]
            key_group = key_heads[:, head_start:head_end]
            scores = score_block(query_block, key_group, block_start)
            weights = jnp.exp(scores - log_totals[number][group])
            grad_weights = jnp.einsum(
                "qhd,khd->hqk",
                grad_block,
                value_heads[:, head_start:head_end],
                preferred_element_type=jnp.float32,
            )
            inner_sum = jnp.sum(weights * grad_weights, -1, keepdims=True)
            grad_scores = (weights * (grad_weights - inner_sum)).astype(jnp.bfloat16)
            query_parts.append(
                jnp.einsum(
                    "hqk,khd->qhd", grad_scores, key_group, preferred_element_type=jnp.float32
                )
                * scaling
            )
            key_sums[group] = (
                key_sums[group]
                + jnp.einsum(
                    "hqk,qhd->khd", grad_scores, query_block, preferred_element_type=jnp.float32
                )
                * scaling
            )
            value_sums[group] = value_sums[group] + jnp.einsum(
                "hqk,qhd->khd",
                weights.astype(jnp.bfloat16),
                grad_block,
                preferred_element_type=jnp.float32,
            )
        grad_queries.append(jnp.concatenate(query_parts, 1))
    return (
        jnp.concatenate(grad_queries, 0),
        jnp.concatenate(key_sums, 1),
        jnp.concatenate(value_sums, 1),
    )


def on_device(
    pixels,
    counts,
    token_ids,
    action_bins,
    patch_pos,
    token_table,
    pos_table,
    w_patch,
    w_res_a,
    w_res_b,
    gain_one,
    bias_one,
    w_q,
    w_k,
    w_v,
    w_o,
    gain_two,
    bias_two,
    w_up,
    w_down,
    cotangent,
):
    length = pixels.shape[0]
    model_width = w_q.shape[0]
    head_count = model_width // HEAD_DIM
    positions = jnp.arange(length)
    image_rows = positions < counts[0, 0]
    action_rows = positions >= length - counts[0, 1]
    table_rows = jnp.logical_not(image_rows)
    row_ids = jnp.where(action_rows, TEXT_VOCAB + action_bins, token_ids)
    rows_owned = token_table.shape[0]
    owners_total = lax.axis_size("emb")
    capacity = 3 * length // (2 * owners_total)
    owner_index = row_ids // rows_owned
    local_row = row_ids - owner_index * rows_owned
    owner_hot = (
        (owner_index[:, None] == jnp.arange(owners_total)[None, :]) & table_rows[:, None]
    ).astype(jnp.int32)
    earlier = jnp.cumsum(owner_hot, 0) - owner_hot
    rank_within = jnp.sum(earlier * owner_hot, 1)
    slot_index = jnp.where(
        table_rows, owner_index * capacity + rank_within, owners_total * capacity
    )
    request = (
        jnp.full((owners_total * capacity + 1,), -1, jnp.int32)
        .at[slot_index]
        .set(jnp.where(table_rows, local_row, -1))
    )
    received = lax.all_to_all(
        request[:-1].reshape(owners_total, capacity), "emb", split_axis=0, concat_axis=0, tiled=True
    )
    valid_slots = received >= 0
    local_ids = jnp.maximum(received, 0)
    fetched = jnp.where(valid_slots[..., None], token_table[local_ids], jnp.zeros((), jnp.bfloat16))
    returned = lax.all_to_all(fetched, "emb", split_axis=0, concat_axis=0, tiled=True)
    slot_safe = jnp.minimum(slot_index, owners_total * capacity - 1)
    table_embed = returned.reshape(owners_total * capacity, model_width)[slot_safe].astype(
        jnp.float32
    )
    patch_first = product(pixels, w_patch)
    first_low = patch_first.astype(jnp.bfloat16)
    res_inner = product(first_low, w_res_a)
    res_gelu, gelu_back_res = jax.vjp(jax.nn.gelu, res_inner)
    res_act = res_gelu.astype(jnp.bfloat16)
    res_mixed = product(res_act, w_res_b)
    position_hot = patch_pos[:, None] == jnp.arange(pos_table.shape[0])[None, :]
    position_embed = product(position_hot.astype(jnp.bfloat16), pos_table)
    image_embed = patch_first + res_mixed + position_embed
    embedded = jnp.where(image_rows[:, None], image_embed, table_embed)
    normed_one_f, norm_back_one = jax.vjp(
        norm_affine, embedded, gain_one.astype(jnp.float32), bias_one.astype(jnp.float32)
    )
    normed_one = normed_one_f.astype(jnp.bfloat16)
    queries = product(normed_one, w_q).astype(jnp.bfloat16).reshape(length, head_count, HEAD_DIM)
    key_heads = product(normed_one, w_k).astype(jnp.bfloat16).reshape(length, head_count, HEAD_DIM)
    value_heads = (
        product(normed_one, w_v).astype(jnp.bfloat16).reshape(length, head_count, HEAD_DIM)
    )
    attended_f, log_totals = attention_forward(queries, key_heads, value_heads)
    attended = attended_f.reshape(length, model_width).astype(jnp.bfloat16)
    middle = embedded + product(attended, w_o)
    normed_two_f, norm_back_two = jax.vjp(
        norm_affine, middle, gain_two.astype(jnp.float32), bias_two.astype(jnp.float32)
    )
    normed_two = normed_two_f.astype(jnp.bfloat16)
    up_pre = product(normed_two, w_up)
    up_act, gelu_back_up = jax.vjp(jax.nn.gelu, up_pre)
    up_low = up_act.astype(jnp.bfloat16)
    output = (middle + product(up_low, w_down)).astype(jnp.bfloat16)
    grad_w_down = product_left(up_low, cotangent)
    (grad_up_pre,) = gelu_back_up(product_right(cotangent, w_down))
    grad_up = grad_up_pre.astype(jnp.bfloat16)
    grad_w_up = product_left(normed_two, grad_up)
    grad_normed_two = product_right(grad_up, w_up)
    grad_middle_norm, grad_gain_two, grad_bias_two = norm_back_two(grad_normed_two)
    grad_middle = cotangent.astype(jnp.float32) + grad_middle_norm
    grad_branch = grad_middle.astype(jnp.bfloat16)
    grad_w_o = product_left(attended, grad_branch)
    grad_attended = (
        product_right(grad_branch, w_o).astype(jnp.bfloat16).reshape(length, head_count, HEAD_DIM)
    )
    grad_queries, grad_keys, grad_values = attention_backward(
        queries, key_heads, value_heads, grad_attended, log_totals
    )
    grad_query_low = grad_queries.reshape(length, model_width).astype(jnp.bfloat16)
    grad_key_low = grad_keys.reshape(length, model_width).astype(jnp.bfloat16)
    grad_value_low = grad_values.reshape(length, model_width).astype(jnp.bfloat16)
    grad_w_q = product_left(normed_one, grad_query_low)
    grad_w_k = product_left(normed_one, grad_key_low)
    grad_w_v = product_left(normed_one, grad_value_low)
    grad_normed_one = (
        product_right(grad_query_low, w_q)
        + product_right(grad_key_low, w_k)
        + product_right(grad_value_low, w_v)
    )
    grad_embed_norm, grad_gain_one, grad_bias_one = norm_back_one(grad_normed_one)
    grad_embedded = grad_middle + grad_embed_norm
    grad_image = jnp.where(image_rows[:, None], grad_embedded, 0.0)
    grad_pos_table = lax.dot_general(
        position_hot.astype(jnp.float32),
        grad_image,
        (((0,), (0,)), ((), ())),
        precision=exact_precision,
    )
    grad_rows = jnp.where(image_rows[:, None], 0.0, grad_embedded).astype(jnp.bfloat16)
    outgoing = (
        jnp.zeros((owners_total * capacity + 1, model_width), jnp.bfloat16)
        .at[slot_index]
        .set(grad_rows)
    )
    incoming = lax.all_to_all(
        outgoing[:-1].reshape(owners_total, capacity, model_width),
        "emb",
        split_axis=0,
        concat_axis=0,
        tiled=True,
    )
    incoming_rows = jnp.where(
        valid_slots.reshape(-1)[:, None], incoming.reshape(-1, model_width).astype(jnp.float32), 0.0
    )
    table_grad = (
        jnp.zeros((rows_owned, model_width), jnp.float32)
        .at[local_ids.reshape(-1)]
        .add(incoming_rows)
    )
    grad_table = lax.psum_scatter(
        table_grad.astype(jnp.bfloat16), "dp", scatter_dimension=1, tiled=True
    ).astype(jnp.float32)
    grad_mixed = grad_image.astype(jnp.bfloat16)
    grad_w_res_b = product_left(res_act, grad_mixed)
    (grad_inner_f,) = gelu_back_res(product_right(grad_mixed, w_res_b))
    grad_inner = grad_inner_f.astype(jnp.bfloat16)
    grad_w_res_a = product_left(first_low, grad_inner)
    grad_first = (grad_image + product_right(grad_inner, w_res_a)).astype(jnp.bfloat16)
    grad_w_patch = product_left(pixels, grad_first)
    grad_pixels = product_right(grad_first, w_patch)
    halfway = (
        lax.psum_scatter(
            grad_pos_table.astype(jnp.bfloat16), "dp", scatter_dimension=0, tiled=True
        ).astype(jnp.float32),
        lax.psum_scatter(
            grad_w_patch.astype(jnp.bfloat16), "dp", scatter_dimension=0, tiled=True
        ).astype(jnp.float32),
        lax.psum_scatter(
            grad_w_res_a.astype(jnp.bfloat16), "dp", scatter_dimension=0, tiled=True
        ).astype(jnp.float32),
        lax.psum_scatter(
            grad_w_res_b.astype(jnp.bfloat16), "dp", scatter_dimension=0, tiled=True
        ).astype(jnp.float32),
        lax.psum_scatter(
            grad_gain_one.astype(jnp.bfloat16), "dp", scatter_dimension=0, tiled=True
        ).astype(jnp.float32),
        lax.psum_scatter(
            grad_bias_one.astype(jnp.bfloat16), "dp", scatter_dimension=0, tiled=True
        ).astype(jnp.float32),
        lax.psum_scatter(
            grad_w_q.astype(jnp.bfloat16), "dp", scatter_dimension=0, tiled=True
        ).astype(jnp.float32),
        lax.psum_scatter(
            grad_w_k.astype(jnp.bfloat16), "dp", scatter_dimension=0, tiled=True
        ).astype(jnp.float32),
        lax.psum_scatter(
            grad_w_v.astype(jnp.bfloat16), "dp", scatter_dimension=0, tiled=True
        ).astype(jnp.float32),
        lax.psum_scatter(
            grad_w_o.astype(jnp.bfloat16), "dp", scatter_dimension=0, tiled=True
        ).astype(jnp.float32),
        lax.psum_scatter(
            grad_gain_two.astype(jnp.bfloat16), "dp", scatter_dimension=0, tiled=True
        ).astype(jnp.float32),
        lax.psum_scatter(
            grad_bias_two.astype(jnp.bfloat16), "dp", scatter_dimension=0, tiled=True
        ).astype(jnp.float32),
        lax.psum_scatter(
            grad_w_up.astype(jnp.bfloat16), "dp", scatter_dimension=0, tiled=True
        ).astype(jnp.float32),
        lax.psum_scatter(
            grad_w_down.astype(jnp.bfloat16), "dp", scatter_dimension=0, tiled=True
        ).astype(jnp.float32),
    )
    shares = (
        lax.psum_scatter(
            halfway[0].astype(jnp.bfloat16), "emb", scatter_dimension=0, tiled=True
        ).astype(jnp.float32),
        lax.psum_scatter(
            halfway[1].astype(jnp.bfloat16), "emb", scatter_dimension=0, tiled=True
        ).astype(jnp.float32),
        lax.psum_scatter(
            halfway[2].astype(jnp.bfloat16), "emb", scatter_dimension=0, tiled=True
        ).astype(jnp.float32),
        lax.psum_scatter(
            halfway[3].astype(jnp.bfloat16), "emb", scatter_dimension=0, tiled=True
        ).astype(jnp.float32),
        lax.psum_scatter(
            halfway[4].astype(jnp.bfloat16), "emb", scatter_dimension=0, tiled=True
        ).astype(jnp.float32),
        lax.psum_scatter(
            halfway[5].astype(jnp.bfloat16), "emb", scatter_dimension=0, tiled=True
        ).astype(jnp.float32),
        lax.psum_scatter(
            halfway[6].astype(jnp.bfloat16), "emb", scatter_dimension=0, tiled=True
        ).astype(jnp.float32),
        lax.psum_scatter(
            halfway[7].astype(jnp.bfloat16), "emb", scatter_dimension=0, tiled=True
        ).astype(jnp.float32),
        lax.psum_scatter(
            halfway[8].astype(jnp.bfloat16), "emb", scatter_dimension=0, tiled=True
        ).astype(jnp.float32),
        lax.psum_scatter(
            halfway[9].astype(jnp.bfloat16), "emb", scatter_dimension=0, tiled=True
        ).astype(jnp.float32),
        lax.psum_scatter(
            halfway[10].astype(jnp.bfloat16), "emb", scatter_dimension=0, tiled=True
        ).astype(jnp.float32),
        lax.psum_scatter(
            halfway[11].astype(jnp.bfloat16), "emb", scatter_dimension=0, tiled=True
        ).astype(jnp.float32),
        lax.psum_scatter(
            halfway[12].astype(jnp.bfloat16), "emb", scatter_dimension=0, tiled=True
        ).astype(jnp.float32),
        lax.psum_scatter(
            halfway[13].astype(jnp.bfloat16), "emb", scatter_dimension=0, tiled=True
        ).astype(jnp.float32),
    )
    return (
        output,
        grad_pixels,
        grad_table,
        shares[0],
        shares[1],
        shares[2],
        shares[3],
        shares[4],
        shares[5],
        shares[6],
        shares[7],
        shares[8],
        shares[9],
        shares[10],
        shares[11],
        shares[12],
        shares[13],
    )


def solution(mesh):
    in_specs = (
        P(("dp", "emb"), None),
        P(("dp", "emb"), None),
        P(("dp", "emb")),
        P(("dp", "emb")),
        P(("dp", "emb")),
        P("emb", None),
        P(),
        P(),
        P(),
        P(),
        P(),
        P(),
        P(),
        P(),
        P(),
        P(),
        P(),
        P(),
        P(),
        P(),
        P(("dp", "emb"), None),
    )
    out_specs = (
        P(("dp", "emb"), None),
        P(("dp", "emb"), None),
        P("emb", "dp"),
        P(("dp", "emb"), None),
        P(("dp", "emb"), None),
        P(("dp", "emb"), None),
        P(("dp", "emb"), None),
        P(("dp", "emb")),
        P(("dp", "emb")),
        P(("dp", "emb"), None),
        P(("dp", "emb"), None),
        P(("dp", "emb"), None),
        P(("dp", "emb"), None),
        P(("dp", "emb")),
        P(("dp", "emb")),
        P(("dp", "emb"), None),
        P(("dp", "emb"), None),
    )
    return jax.shard_map(
        on_device, mesh=mesh, in_specs=in_specs, out_specs=out_specs, check_vma=False
    )
```

profile of v0, /device:TPU:1, one launch (start us, length us, event | category | flops | bytes accessed | tf_op | source)
XLA Modules:
  0.0 1503.0 jit_solution(3119808432593578272)
XLA Ops:
  117.0 17.8 %fusion.33 = (f32[12,512]{1,0:T(8,128)S(1)}, f32[12,512]{1,0:T(8,128)S(1)}, f32[12,512,1024]{2,1,0:T(8,128)}) fusion(pred[512,1024]{1,0:T(8,128)(4,1)S(1)} %iota_compare_fusion, f32[12,512,1024]{2,1,0:T(8,128)} %fusion.97, bf16[1024,24,32]{0,2,1:T(8,128)(2,1)} %bitcast.148, bf16[1024,24,32]{0,2,1:T(8,128)(2,1)} %bitcast.156), kind=kOutput, calls=%fused_computation.61 | convolution fusion | flops 440389632 | bytes 52084736 | tf_op jit(solution)/shard_map/qhd,khd->hqk/dot_general | solution.py:41
  134.7 20.0 %fusion.2 = (f32[12,512]{1,0:T(8,128)S(1)}, f32[12,512]{1,0:T(8,128)S(1)}) fusion(f32[12,512]{1,0:T(8,128)S(1)} %get-tuple-element.101, f32[12,512,1024]{2,1,0:T(8,128)} %get-tuple-element.127, pred[512,1024]{1,0:T(8,128)(4,1)S(1)} %iota_compare_fusion, f32[12,512]{1,0:T(8,128)S(1)} %get-tuple-element.102, f32[12,512,1024]{2,1,0:T(8,128)} %fusion.97), kind=kLoop, calls=%fused_computation.31 | loop fusion | flops 50319360 | bytes 50954240 | tf_op jit(solution)/shard_map/reduce_sum | solution.py:69
  166.9 17.7 %fusion.31 = (f32[12,512]{1,0:T(8,128)S(1)}, f32[12,512]{1,0:T(8,128)S(1)}, f32[12,512,1024]{2,1,0:T(8,128)}) fusion(pred[512,1024]{1,0:T(8,128)(4,1)S(1)} %iota_compare_fusion.1, f32[12,512,1024]{2,1,0:T(8,128)} %fusion.99, bf16[1024,24,32]{0,2,1:T(8,128)(2,1)} %bitcast.149, bf16[1024,24,32]{0,2,1:T(8,128)(2,1)} %bitcast.157), kind=kOutput, calls=%fused_computation.59 | convolution fusion | flops 440389632 | bytes 52084736 | tf_op jit(solution)/shard_map/qhd,khd->hqk/dot_general | solution.py:41
  184.7 21.5 %fusion = (f32[12,512]{1,0:T(8,128)S(1)}, f32[12,512]{1,0:T(8,128)S(1)}) fusion(f32[12,512]{1,0:T(8,128)S(1)} %get-tuple-element.97, f32[12,512,1024]{2,1,0:T(8,128)} %get-tuple-element.128, pred[512,1024]{1,0:T(8,128)(4,1)S(1)} %iota_compare_fusion.1, f32[12,512]{1,0:T(8,128)S(1)} %get-tuple-element.98, f32[12,512,1024]{2,1,0:T(8,128)} %fusion.99), kind=kLoop, calls=%fused_computation.29 | loop fusion | flops 50319360 | bytes 50954240 | tf_op jit(solution)/shard_map/reduce_sum | solution.py:69
  206.3 12.1 fusion.76
  249.8 16.8 %fusion.14 = bf16[1024,3072]{1,0:T(8,128)(2,1)} fusion(f32[1024,3072]{1,0:T(8,128)S(1)} %fusion.162, bf16[1024,768]{1,0:T(8,128)(2,1)S(1)} %copy-done.34, bf16[3072,768]{1,0:T(8,128)(2,1)} %param.40), kind=kOutput, calls=%fused_computation.45 | convolution fusion | flops 4894752768 | bytes 25165824 | tf_op jit(solution)/shard_map/dot_general | solution.py:35
  311.0 35.5 %multiply_reduce_fusion.3 = (f32[12,512]{1,0:T(8,128)S(1)}, f32[12,512]{1,0:T(8,128)S(1)}, f32[12,512,1024]{2,1,0:T(8,128)}) fusion(f32[12,512]{1,0:T(8,128)S(1)} %log_add_fusion.3, f32[12,512,1024]{2,1,0:T(8,128)} %get-tuple-element.128, pred[512,1024]{1,0:T(8,128)(4,1)S(1)} %iota_compare_fusion.1, f32[12,512,1024]{2,1,0:T(8,128)} %fusion.89, ...), kind=kOutput, calls=%fused_computation.15 | convolution fusion | flops 465555456 | bytes 102465536 | tf_op jit(solution)/shard_map/qhd,khd->hqk/dot_general | solution.py:109
  346.5 41.9 %multiply_convert_fusion.3 = (bf16[12,512,1024]{2,1,0:T(8,128)(2,1)}, bf16[12,512,1024]{2,1,0:T(8,128)(2,1)}) fusion(f32[12,512,1024]{2,1,0:T(8,128)} %get-tuple-element.132, f32[12,512]{1,0:T(8,128)S(1)} %get-tuple-element.91, f32[12,512]{1,0:T(8,128)S(1)} %log_add_fusion.3, f32[12,512,1024]{2,1,0:T(8,128)} %get-tuple-element.128, ...), kind=kLoop, calls=%fused_computation.14 | loop fusion | flops 75497472 | bytes 126451712 | tf_op jit(solution)/shard_map/convert_element_type | solution.py:116
  427.0 12.8 fusion.61
  451.0 12.4 fusion.58
  463.4 35.4 %multiply_reduce_fusion.1 = (f32[12,512]{1,0:T(8,128)S(1)}, f32[12,512]{1,0:T(8,128)S(1)}, f32[12,512,1024]{2,1,0:T(8,128)}) fusion(f32[12,512]{1,0:T(8,128)S(1)} %copy-done.54, f32[12,512,1024]{2,1,0:T(8,128)} %get-tuple-element.127, pred[512,1024]{1,0:T(8,128)(4,1)S(1)} %copy-done.16, f32[12,512,1024]{2,1,0:T(8,128)} %fusion.91, ...), kind=kOutput, calls=%fused_computation.9 | convolution fusion | flops 465555456 | bytes 102465536 | tf_op jit(solution)/shard_map/qhd,khd->hqk/dot_general | solution.py:109
  498.9 41.9 %multiply_convert_fusion.1 = (bf16[12,512,1024]{2,1,0:T(8,128)(2,1)}, bf16[12,512,1024]{2,1,0:T(8,128)(2,1)}) fusion(f32[12,512,1024]{2,1,0:T(8,128)} %get-tuple-element.131, f32[12,512]{1,0:T(8,128)S(1)} %get-tuple-element.93, f32[12,512]{1,0:T(8,128)S(1)} %copy-done.54, f32[12,512,1024]{2,1,0:T(8,128)} %get-tuple-element.127, ...), kind=kLoop, calls=%fused_computation.8 | loop fusion | flops 75497472 | bytes 126451712 | tf_op jit(solution)/shard_map/convert_element_type | solution.py:116
  640.7 12.1 convolution_convert_fusion
  654.1 20.2 %reduce-scatter.32.cloned.1.call-done = bf16[192,768]{1,0:T(8,128)(2,1)} async-done(((bf16[768,768]{1,0:T(8,128)(2,1)}), bf16[192,768]{1,0:T(8,128)(2,1)}) %reduce-scatter.32.cloned.1.call-update) | async-done | bytes 294928 | tf_op jit(solution)/shard_map/reduce_scatter | solution.py:308
  674.4 30.7 %reduce-scatter.36.cloned.1.call-done = bf16[192,768]{1,0:T(8,128)(2,1)} async-done(((bf16[768,768]{1,0:T(8,128)(2,1)}), bf16[192,768]{1,0:T(8,128)(2,1)}) %reduce-scatter.36.cloned.1.call-update) | async-done | bytes 294928 | tf_op jit(solution)/shard_map/reduce_scatter | solution.py:311
  705.2 30.7 %reduce-scatter.40.cloned.1.call-done = bf16[192,768]{1,0:T(8,128)(2,1)} async-done(((bf16[768,768]{1,0:T(8,128)(2,1)}), bf16[192,768]{1,0:T(8,128)(2,1)}) %reduce-scatter.40.cloned.1.call-update) | async-done | bytes 294928 | tf_op jit(solution)/shard_map/reduce_scatter | solution.py:320
  735.9 30.7 %reduce-scatter.44.cloned.1.call-done = bf16[192,768]{1,0:T(8,128)(2,1)} async-done(((bf16[768,768]{1,0:T(8,128)(2,1)}), bf16[192,768]{1,0:T(8,128)(2,1)}) %reduce-scatter.44.cloned.1.call-update) | async-done | bytes 294928 | tf_op jit(solution)/shard_map/reduce_scatter | solution.py:323
  766.7 30.3 %reduce-scatter.48.cloned.1.call-done = bf16[192,768]{1,0:T(8,128)(2,1)} async-done(((bf16[768,768]{1,0:T(8,128)(2,1)}), bf16[192,768]{1,0:T(8,128)(2,1)}) %reduce-scatter.48.cloned.1.call-update) | async-done | bytes 294928 | tf_op jit(solution)/shard_map/reduce_scatter | solution.py:326
  797.1 30.3 %reduce-scatter.52.cloned.1.call-done = bf16[192,768]{1,0:T(8,128)(2,1)} async-done(((bf16[768,768]{1,0:T(8,128)(2,1)}), bf16[192,768]{1,0:T(8,128)(2,1)}) %reduce-scatter.52.cloned.1.call-update) | async-done | bytes 294928 | tf_op jit(solution)/shard_map/reduce_scatter | solution.py:329
  827.4 86.6 %reduce-scatter.56.cloned.1.call-done = bf16[192,3072]{1,0:T(8,128)(2,1)} async-done(((bf16[768,3072]{1,0:T(8,128)(2,1)}), bf16[192,3072]{1,0:T(8,128)(2,1)}) %reduce-scatter.56.cloned.1.call-update) | async-done | bytes 1179664 | tf_op jit(solution)/shard_map/reduce_scatter | solution.py:338
  931.5 70.5 %reduce-scatter.60.cloned.1.call-done = bf16[768,768]{1,0:T(8,128)(2,1)} async-done(((bf16[3072,768]{1,0:T(8,128)(2,1)}), bf16[768,768]{1,0:T(8,128)(2,1)}) %reduce-scatter.60.cloned.1.call-update) | async-done | bytes 1179664 | tf_op jit(solution)/shard_map/reduce_scatter | solution.py:341
  1002.4 17.6 %scatter_custom_fusion.2 = f32[4128,768]{1,0:T(8,128)} fusion(s32[1536]{0:T(1024)} %copy-done.68, f32[]{:T(128)} %constant.21.clone.1, bf16[1536,768]{1,0:T(8,128)(2,1)} %bitcast.34, pred[1536]{0:T(1024)(128)(4,1)S(1)} %ge.27), kind=kCustom, calls=%fused_computation.63 | custom fusion | flops 3538944 | bytes 15043072 | tf_op jit(solution)/shard_map/scatter-add | solution.py:288
  1062.1 14.1 all-reduce.8
  1086.4 23.7 %reduce-scatter.34.cloned.1.call-done = bf16[24,768]{1,0:T(8,128)(2,1)} async-done(((bf16[192,768]{1,0:T(8,128)(2,1)}), bf16[24,768]{1,0:T(8,128)(2,1)}) %reduce-scatter.34.cloned.1.call-update) | async-done | bytes 36880 | tf_op jit(solution)/shard_map/reduce_scatter | solution.py:352
  1111.6 34.7 %reduce-scatter.38.cloned.1.call-done = bf16[24,768]{1,0:T(8,128)(2,1)} async-done(((bf16[192,768]{1,0:T(8,128)(2,1)}), bf16[24,768]{1,0:T(8,128)(2,1)}) %reduce-scatter.38.cloned.1.call-update) | async-done | bytes 36880 | tf_op jit(solution)/shard_map/reduce_scatter | solution.py:355
  1147.7 34.7 %reduce-scatter.42.cloned.1.call-done = bf16[24,768]{1,0:T(8,128)(2,1)} async-done(((bf16[192,768]{1,0:T(8,128)(2,1)}), bf16[24,768]{1,0:T(8,128)(2,1)}) %reduce-scatter.42.cloned.1.call-update) | async-done | bytes 36880 | tf_op jit(solution)/shard_map/reduce_scatter | solution.py:364
  1183.8 34.7 %reduce-scatter.46.cloned.1.call-done = bf16[24,768]{1,0:T(8,128)(2,1)} async-done(((bf16[192,768]{1,0:T(8,128)(2,1)}), bf16[24,768]{1,0:T(8,128)(2,1)}) %reduce-scatter.46.cloned.1.call-update) | async-done | bytes 36880 | tf_op jit(solution)/shard_map/reduce_scatter | solution.py:367
  1219.9 34.7 %reduce-scatter.50.cloned.1.call-done = bf16[24,768]{1,0:T(8,128)(2,1)} async-done(((bf16[192,768]{1,0:T(8,128)(2,1)}), bf16[24,768]{1,0:T(8,128)(2,1)}) %reduce-scatter.50.cloned.1.call-update) | async-done | bytes 36880 | tf_op jit(solution)/shard_map/reduce_scatter | solution.py:370
  1256.0 34.7 %reduce-scatter.54.cloned.1.call-done = bf16[24,768]{1,0:T(8,128)(2,1)} async-done(((bf16[192,768]{1,0:T(8,128)(2,1)}), bf16[24,768]{1,0:T(8,128)(2,1)}) %reduce-scatter.54.cloned.1.call-update) | async-done | bytes 36880 | tf_op jit(solution)/shard_map/reduce_scatter | solution.py:373
  1292.1 39.3 %reduce-scatter.58.cloned.1.call-done = bf16[24,3072]{1,0:T(8,128)(2,1)} async-done(((bf16[192,3072]{1,0:T(8,128)(2,1)}), bf16[24,3072]{1,0:T(8,128)(2,1)}) %reduce-scatter.58.cloned.1.call-update) | async-done | bytes 147472 | tf_op jit(solution)/shard_map/reduce_scatter | solution.py:382
  1333.1 38.2 %reduce-scatter.62.cloned.1.call-done = bf16[96,768]{1,0:T(8,128)(2,1)} async-done(((bf16[768,768]{1,0:T(8,128)(2,1)}), bf16[96,768]{1,0:T(8,128)(2,1)}) %reduce-scatter.62.cloned.1.call-update) | async-done | bytes 147472 | tf_op jit(solution)/shard_map/reduce_scatter | solution.py:385
  1372.9 114.9 %reduce-scatter.64.cloned.1.call-done = bf16[192,4128]{1,0:T(8,128)(2,1)} async-done(((bf16[768,4128]{1,0:T(8,128)(2,1)}), bf16[192,4128]{1,0:T(8,128)(2,1)}) %reduce-scatter.64.cloned.1.call-update) | async-done | bytes 1585168
  (386 shorter events, 436.0 us)
Async XLA Ops:
  7.2 44.2 %copy-start = (bf16[1024,768]{1,0:T(8,128)(2,1)S(1)}, bf16[1024,768]{1,0:T(8,128)(2,1)}, u32[]{:S(2)}) copy-start(bf16[1024,768]{1,0:T(8,128)(2,1)} %param.21) | copy-start | bytes 4718596
  9.9 74.0 %copy-start.71 = (pred[1024]{0:T(1024)(128)(4,1)}, pred[1024]{0:T(1024)(128)(4,1)S(1)}, u32[]{:S(2)}) copy-start(pred[1024]{0:T(1024)(128)(4,1)S(1)} %get-tuple-element.136) | copy-start | bytes 3076
  42.7 31.1 %all-to-all-start.1 = ((bf16[8,192,768]{2,1,0:T(8,128)(2,1)}), bf16[8,192,768]{2,1,0:T(8,128)(2,1)}, u32[]{:S(2)}, u32[]{:S(2)}) async-start(bf16[8,192,768]{2,1,0:T(8,128)(2,1)} %broadcast_select_fusion), calls=%async_computation.1 | async-start | bytes 4718592 | tf_op jit(solution)/shard_map/all_to_all | solution.py:199
  47.8 605.1 %reduce-scatter.28.cloned.1.call-start = ((), (), s32[]{:S(2)}) async-start(), calls=%async_computation.24 | async-start | bytes 491520 | tf_op jit(solution)/shard_map/reduce_scatter | solution.py:302
  48.0 40.6 %copy-start.60 = (f32[768]{0:T(1024)}, f32[768]{0:T(1024)S(1)}, u32[]{:S(2)}) copy-start(f32[768]{0:T(1024)S(1)} %convert_element_type.259) | copy-start | bytes 9220
  51.0 295.4 %copy-start.17 = (pred[512,1024]{1,0:T(8,128)(4,1)}, pred[512,1024]{1,0:T(8,128)(4,1)S(1)}, u32[]{:S(2)}) copy-start(pred[512,1024]{1,0:T(8,128)(4,1)S(1)} %iota_compare_fusion.1) | copy-start | bytes 1572868
  51.4 167.6 %copy-start.14 = (pred[512,1024]{1,0:T(8,128)(4,1)}, pred[512,1024]{1,0:T(8,128)(4,1)S(1)}, u32[]{:S(2)}) copy-start(pred[512,1024]{1,0:T(8,128)(4,1)S(1)} %iota_compare_fusion) | copy-start | bytes 1572868
  242.4 42.6 %copy-start.44 = (f32[1024]{0:T(1024)}, f32[1024]{0:T(1024)S(1)}, u32[]{:S(2)}) copy-start(f32[1024]{0:T(1024)S(1)} %broadcast_multiply_fusion) | copy-start | bytes 12292
  244.1 40.9 %copy-start.48 = (f32[1024]{0:T(1024)}, f32[1024]{0:T(1024)S(1)}, u32[]{:S(2)}) copy-start(f32[1024]{0:T(1024)S(1)} %fusion.139) | copy-start | bytes 12292
  346.5 41.9 %copy-start.23 = (bf16[1024,768]{0,1:T(8,128)(2,1)S(1)}, bf16[1024,768]{0,1:T(8,128)(2,1)}, u32[]{:S(2)}) copy-start(bf16[1024,768]{0,1:T(8,128)(2,1)} %copy-done.22) | copy-start | bytes 4718596
  591.1 62.5 %reduce-scatter.66.cloned.1.call-start = ((), (), s32[]{:S(2)}) async-start(), calls=%async_computation.43 | async-start | bytes 1474560
  601.3 73.0 %reduce-scatter.32.cloned.1.call-start = ((), (), s32[]{:S(2)}) async-start(), calls=%async_computation.26 | async-start | bytes 1474560 | tf_op jit(solution)/shard_map/reduce_scatter | solution.py:308
  606.1 99.0 %reduce-scatter.36.cloned.1.call-start = ((), (), s32[]{:S(2)}) async-start(), calls=%async_computation.28 | async-start | bytes 1474560 | tf_op jit(solution)/shard_map/reduce_scatter | solution.py:311
  612.7 123.1 %reduce-scatter.40.cloned.1.call-start = ((), (), s32[]{:S(2)}) async-start(), calls=%async_computation.30 | async-start | bytes 1474560 | tf_op jit(solution)/shard_map/reduce_scatter | solution.py:320
  617.1 149.5 %reduce-scatter.44.cloned.1.call-start = ((), (), s32[]{:S(2)}) async-start(), calls=%async_computation.32 | async-start | bytes 1474560 | tf_op jit(solution)/shard_map/reduce_scatter | solution.py:323
  621.5 175.5 %reduce-scatter.48.cloned.1.call-start = ((), (), s32[]{:S(2)}) async-start(), calls=%async_computation.34 | async-start | bytes 1474560 | tf_op jit(solution)/shard_map/reduce_scatter | solution.py:326
  626.0 201.3 %reduce-scatter.52.cloned.1.call-start = ((), (), s32[]{:S(2)}) async-start(), calls=%async_computation.36 | async-start | bytes 1474560 | tf_op jit(solution)/shard_map/reduce_scatter | solution.py:329
  630.5 283.5 %reduce-scatter.56.cloned.1.call-start = ((), (), s32[]{:S(2)}) async-start(), calls=%async_computation.38 | async-start | bytes 5898240 | tf_op jit(solution)/shard_map/reduce_scatter | solution.py:338
  640.4 361.6 %reduce-scatter.60.cloned.1.call-start = ((), (), s32[]{:S(2)}) async-start(), calls=%async_computation.40 | async-start | bytes 5898240 | tf_op jit(solution)/shard_map/reduce_scatter | solution.py:341
  652.8 430.6 %reduce-scatter.30.cloned.1.call-start = ((), (), s32[]{:S(2)}) async-start(), calls=%async_computation.25 | async-start | bytes 110592 | tf_op jit(solution)/shard_map/reduce_scatter | solution.py:346
  653.5 431.2 %reduce-scatter.68.cloned.1.call-start = ((), (), s32[]{:S(2)}) async-start(), calls=%async_computation.44 | async-start | bytes 331776
  654.1 456.1 %reduce-scatter.34.cloned.1.call-start = ((), (), s32[]{:S(2)}) async-start(), calls=%async_computation.27 | async-start | bytes 331776 | tf_op jit(solution)/shard_map/reduce_scatter | solution.py:352
  674.4 471.9 %reduce-scatter.38.cloned.1.call-start = ((), (), s32[]{:S(2)}) async-start(), calls=%async_computation.29 | async-start | bytes 331776 | tf_op jit(solution)/shard_map/reduce_scatter | solution.py:355
  705.1 477.2 %reduce-scatter.42.cloned.1.call-start = ((), (), s32[]{:S(2)}) async-start(), calls=%async_computation.31 | async-start | bytes 331776 | tf_op jit(solution)/shard_map/reduce_scatter | solution.py:364
  735.9 482.6 %reduce-scatter.46.cloned.1.call-start = ((), (), s32[]{:S(2)}) async-start(), calls=%async_computation.33 | async-start | bytes 331776 | tf_op jit(solution)/shard_map/reduce_scatter | solution.py:367
  766.7 487.9 %reduce-scatter.50.cloned.1.call-start = ((), (), s32[]{:S(2)}) async-start(), calls=%async_computation.35 | async-start | bytes 331776 | tf_op jit(solution)/shard_map/reduce_scatter | solution.py:370
  797.0 493.7 %reduce-scatter.54.cloned.1.call-start = ((), (), s32[]{:S(2)}) async-start(), calls=%async_computation.37 | async-start | bytes 331776 | tf_op jit(solution)/shard_map/reduce_scatter | solution.py:373
  827.4 504.0 %reduce-scatter.58.cloned.1.call-start = ((), (), s32[]{:S(2)}) async-start(), calls=%async_computation.39 | async-start | bytes 1327104 | tf_op jit(solution)/shard_map/reduce_scatter | solution.py:382
  926.7 75.6 %copy-start.59 = (s32[8,1,192]{2,1,0:T(1,128)S(1)}, s32[8,1,192]{2,1,0:T(1,128)}, u32[]{:S(2)}) copy-start(s32[8,1,192]{2,1,0:T(1,128)} %copy-done.58) | copy-start | bytes 18436
  926.7 75.8 %all-to-all-start.2 = ((bf16[8,192,768]{2,1,0:T(8,128)(2,1)}), bf16[8,192,768]{2,1,0:T(8,128)(2,1)}, u32[]{:S(2)}, u32[]{:S(2)}) async-start(bf16[8,192,768]{2,1,0:T(8,128)(2,1)} %bitcast.163), calls=%async_computation.2 | async-start | bytes 4718592 | tf_op jit(solution)/shard_map/all_to_all | solution.py:275
  931.5 439.7 %reduce-scatter.62.cloned.1.call-start = ((), (), s32[]{:S(2)}) async-start(), calls=%async_computation.41 | async-start | bytes 1327104 | tf_op jit(solution)/shard_map/reduce_scatter | solution.py:385
  1002.1 485.8 %reduce-scatter.64.cloned.1.call-start = ((), (), s32[]{:S(2)}) async-start(), calls=%async_computation.42 | async-start | bytes 8110080
  (92 other events, 556.2 us)
Sparse Core Ops, SparseCore 0:
  591.2 21.6 reduce-scatter.27
  615.4 28.5 reduce-scatter.65
  646.4 27.8 reduce-scatter.31
  677.2 27.8 reduce-scatter.35
  708.0 27.8 reduce-scatter.39
  738.7 27.8 reduce-scatter.43
  769.1 27.8 reduce-scatter.47
  799.4 27.8 reduce-scatter.51
  829.8 84.1 reduce-scatter.55
  916.2 85.7 reduce-scatter.59
  1005.3 32.3 reduce-scatter.29
  1041.0 32.9 reduce-scatter.67
  1077.3 32.8 reduce-scatter.33
  1113.4 32.8 reduce-scatter.37
  1149.5 32.8 reduce-scatter.41
  1185.6 32.8 reduce-scatter.45
  1221.7 32.8 reduce-scatter.49
  1257.8 32.8 reduce-scatter.53
  1294.2 37.1 reduce-scatter.57
  1334.5 36.7 reduce-scatter.61
  1373.7 114.0 reduce-scatter.63
where the time goes:
time: 1510 us; the launch traced here: 1500 us
  waiting for transfers between devices  732 us (48%)
  matrix products  428 us (28%)
  other arithmetic  191 us (13%)
  local copies, waits for them, and re-layouts  89.9 us (6%)
  blocking collectives  32.2 us (2%)
  between operations  17.8 us (1%)
    unnamed x24, waiting for transfers between devices  116 us
    dot_general x4, matrix products, attention_backward(): jnp.einsum('qhd,khd->hqk', grad_block, value_heads[:, head_start:head_end...  91.5 us
    reduce_scatter x1, waiting for transfers between devices, on_device(): lax.psum_scatter(grad_w_up.astype(jnp.bfloat16), 'dp', scatter_dimension=...  86.6 us
    convert_element_type x2, other arithmetic, attention_backward(): grad_scores = (weights * (grad_weights - inner_sum)).astype(jnp.bfloat16)  83.8 us
    reduce_scatter x1, waiting for transfers between devices, on_device(): lax.psum_scatter(grad_w_down.astype(jnp.bfloat16), 'dp', scatter_dimensio...  70.5 us
    dot_general x4, matrix products, score_block(): jnp.einsum('qhd,khd->hqk', query_block, key_heads, preferred_element_type...  56 us
    dot_general x9, matrix products, product_left(): lax.dot_general(left, right, (((0,), (0,)), ((), ())), preferred_element_...  52.6 us
    dot_general x9, matrix products, product_right(): lax.dot_general(left, right, (((1,), (1,)), ((), ())), preferred_element_...  50.3 us
  transfers between devices with their start and end apart: 23, of which 18 were waited for; matrix products, arithmetic and copies ran while one was open for 10% of the time, Pallas kernels for 0%

commit v1 on v0

v1 whole, which is shorter than its diff:
```python
import functools

import jax
import jax.numpy as jnp
from jax import lax
from jax.experimental import pallas as pl
from jax.experimental.pallas import tpu as pltpu
from jax.sharding import PartitionSpec as P

HEAD_DIM = 32
TEXT_VOCAB = 32000
BLOCK = 256
HEADS_STEP = 2
BOTH = ("dp", "emb")
LOG2_E = 1.4426950408889634


def normalize(values):
    average = jnp.mean(values, -1, keepdims=True)
    centred = values - average
    variance = jnp.mean(centred * centred, -1, keepdims=True)
    return centred * lax.rsqrt(variance + 1e-05)


def norm_affine(values, gain, offset):
    return normalize(values) * gain + offset


def contract(left, right, left_dim, right_dim):
    return lax.dot_general(
        left, right, (((left_dim,), (right_dim,)), ((), ())), preferred_element_type=jnp.float32
    )


def product(left, right):
    return contract(left, right, 1, 0)


def product_left(left, right):
    return contract(left, right, 0, 0)


def product_right(left, right):
    return contract(left, right, 1, 1)


def forward_kernel(heads, q_ref, k_ref, v_ref, o_ref, p_ref, r_ref):
    length = q_ref.shape[1]
    scaling = HEAD_DIM ** (-0.5) * LOG2_E
    key_place = lax.broadcasted_iota(jnp.int32, (BLOCK, BLOCK), 0)
    query_place = lax.broadcasted_iota(jnp.int32, (BLOCK, BLOCK), 1)
    allowed = key_place <= query_place
    for head in range(heads):
        rows = slice(head * HEAD_DIM, (head + 1) * HEAD_DIM)
        keys = k_ref[rows, :]
        values = v_ref[rows, :]
        for step in range(length // BLOCK):
            start, end = step * BLOCK, (step + 1) * BLOCK
            scores = contract(keys[:, :end], q_ref[rows, start:end], 0, 0) * scaling
            corner = jnp.where(allowed, scores[start:], -1e30)
            highest = jnp.max(corner, 0, keepdims=True)
            if step:
                highest = jnp.maximum(highest, jnp.max(scores[:start], 0, keepdims=True))
            weights = jnp.exp2(corner - highest)
            total = jnp.sum(weights, 0, keepdims=True)
            weights = weights.astype(jnp.bfloat16)
            if step:
                above = jnp.exp2(scores[:start] - highest)
                total = total + jnp.sum(above, 0, keepdims=True)
                weights = jnp.concatenate([above.astype(jnp.bfloat16), weights], 0)
            inverse = 1.0 / total
            base = BLOCK * (step * (step + 1) // 2)
            p_ref[head, base : base + end, :] = weights
            r_ref[head, :, start:end] = inverse
            o_ref[rows, start:end] = (
                contract(values[:, :end], weights, 1, 0) * inverse
            ).astype(jnp.bfloat16)


def packed_rows(length):
    steps = length // BLOCK
    return BLOCK * (steps * (steps + 1) // 2)


def attention_forward(queries, key_heads, values):
    width, length = queries.shape
    heads = width // HEAD_DIM
    packed = packed_rows(length)
    rows = pl.BlockSpec((HEADS_STEP * HEAD_DIM, length), lambda g: (g, 0))
    return pl.pallas_call(
        functools.partial(forward_kernel, HEADS_STEP),
        grid=(heads // HEADS_STEP,),
        in_specs=[rows] * 3,
        out_specs=[
            rows,
            pl.BlockSpec((HEADS_STEP, packed, BLOCK), lambda g: (g, 0, 0)),
            pl.BlockSpec((HEADS_STEP, 1, length), lambda g: (g, 0, 0)),
        ],
        out_shape=[
            jax.ShapeDtypeStruct((width, length), jnp.bfloat16),
            jax.ShapeDtypeStruct((heads, packed, BLOCK), jnp.bfloat16),
            jax.ShapeDtypeStruct((heads, 1, length), jnp.float32),
        ],
        compiler_params=pltpu.CompilerParams(vmem_limit_bytes=32 << 20),
        cost_estimate=pl.CostEstimate(
            flops=50_000_000_000, bytes_accessed=heads * packed * BLOCK * 2, transcendentals=0
        ),
        name="attention_forward",
    )(queries, key_heads, values)


def backward_kernel(heads, q_ref, k_ref, v_ref, o_ref, g_ref, p_ref, r_ref, d_ref, s_ref):
    length = q_ref.shape[1]
    steps = length // BLOCK
    scaling = HEAD_DIM ** (-0.5)
    for head in range(heads):
        rows = slice(head * HEAD_DIM, (head + 1) * HEAD_DIM)
        grads = (g_ref[rows, :].astype(jnp.float32) * r_ref[head]).astype(jnp.bfloat16)
        inner = jnp.sum(
            grads.astype(jnp.float32) * o_ref[rows, :].astype(jnp.float32), 0, keepdims=True
        )
        queries = q_ref[rows, :]
        keys = k_ref[rows, :]
        values = v_ref[rows, :]
        for step in range(steps):
            start, end = step * BLOCK, (step + 1) * BLOCK
            base = BLOCK * (step * (step + 1) // 2)
            grad_probs = contract(values[:, :end], grads[:, start:end], 0, 0)
            grad_scores = p_ref[head, base : base + end, :] * (
                grad_probs - inner[:, start:end]
            ).astype(jnp.bfloat16)
            s_ref[head, base : base + end, :] = grad_scores
            d_ref[0, rows, start:end] = (
                contract(keys[:, :end], grad_scores, 1, 0) * scaling
            ).astype(jnp.bfloat16)
        for column in range(steps):
            grad_keys = jnp.zeros((HEAD_DIM, BLOCK), jnp.float32)
            grad_values = jnp.zeros((HEAD_DIM, BLOCK), jnp.float32)
            for step in range(column, steps):
                base = BLOCK * (step * (step + 1) // 2 + column)
                span = slice(step * BLOCK, (step + 1) * BLOCK)
                grad_values = grad_values + contract(
                    grads[:, span], p_ref[head, base : base + BLOCK, :], 1, 1
                )
                grad_keys = grad_keys + contract(
                    queries[:, span], s_ref[head, base : base + BLOCK, :], 1, 1
                )
            span = slice(column * BLOCK, (column + 1) * BLOCK)
            d_ref[1, rows, span] = (grad_keys * scaling).astype(jnp.bfloat16)
            d_ref[2, rows, span] = grad_values.astype(jnp.bfloat16)


def attention_backward(queries, key_heads, values, attended, grads, probs, inverse):
    width, length = queries.shape
    heads = width // HEAD_DIM
    packed = packed_rows(length)
    rows = pl.BlockSpec((HEADS_STEP * HEAD_DIM, length), lambda g: (g, 0))
    return pl.pallas_call(
        functools.partial(backward_kernel, HEADS_STEP),
        grid=(heads // HEADS_STEP,),
        in_specs=[rows] * 5
        + [
            pl.BlockSpec((HEADS_STEP, packed, BLOCK), lambda g: (g, 0, 0)),
            pl.BlockSpec((HEADS_STEP, 1, length), lambda g: (g, 0, 0)),
        ],
        out_specs=pl.BlockSpec((3, HEADS_STEP * HEAD_DIM, length), lambda g: (0, g, 0)),
        out_shape=jax.ShapeDtypeStruct((3, width, length), jnp.bfloat16),
        scratch_shapes=[pltpu.VMEM((HEADS_STEP, packed, BLOCK), jnp.bfloat16)],
        compiler_params=pltpu.CompilerParams(vmem_limit_bytes=32 << 20),
        cost_estimate=pl.CostEstimate(
            flops=55_000_000_000, bytes_accessed=heads * packed * BLOCK * 2, transcendentals=0
        ),
        name="attention_backward",
    )(queries, key_heads, values, attended, grads, probs, inverse)


def chunk_shape(capacity, columns):
    if columns % 128 == 64 and capacity % 32 == 0:
        return (capacity * columns // 128, 128)
    return (capacity, columns)


def pack_kernel(parts, grad_ref, slot_ref, out_ref):
    length, width = grad_ref.shape
    columns = width // parts
    rows, lanes = out_ref.shape[2:]
    capacity = rows * lanes // columns
    slots = pl.program_id(0) * capacity + lax.broadcasted_iota(
        jnp.int32, (capacity, length), 0
    )
    hot = jnp.where(slots == slot_ref[...], 1.0, 0.0).astype(jnp.bfloat16)
    packed = product(hot, grad_ref[...])
    for part in range(parts):
        start = part * columns
        if lanes == columns:
            out_ref[part, 0] = packed[:, start : start + columns].astype(jnp.bfloat16)
            continue
        full = columns // 128 * 128
        tail = start + full
        for tile in range(full // 128):
            place = start + tile * 128
            if start % 128 == 0:
                piece = packed[:, place : place + 128]
            else:
                left = lax.broadcasted_iota(jnp.int32, (capacity, 128), 1) < 64
                piece = jnp.where(
                    left,
                    pltpu.roll(packed[:, place - 64 : place + 64], 64, 1),
                    pltpu.roll(packed[:, place + 64 : place + 192], 64, 1),
                )
            out_ref[part, 0, tile * capacity : (tile + 1) * capacity, :] = piece.astype(
                jnp.bfloat16
            )
        tile = tail // 128 * 128
        upper = packed[: capacity // 2, tile : tile + 128]
        lower = packed[capacity // 2 :, tile : tile + 128]
        left = lax.broadcasted_iota(jnp.int32, upper.shape, 1) < 64
        if tail % 128 == 0:
            mixed = jnp.where(left, upper, pltpu.roll(lower, 64, 1))
        else:
            mixed = jnp.where(left, pltpu.roll(upper, 64, 1), lower)
        out_ref[part, 0, full // 128 * capacity :, :] = mixed.astype(jnp.bfloat16)


def pack_rows(grad_rows, slot_index, parts, owners, capacity):
    length, width = grad_rows.shape
    rows, lanes = chunk_shape(capacity, width // parts)
    return pl.pallas_call(
        functools.partial(pack_kernel, parts),
        grid=(owners,),
        in_specs=[
            pl.BlockSpec((length, width), lambda o: (0, 0)),
            pl.BlockSpec((1, length), lambda o: (0, 0)),
        ],
        out_specs=pl.BlockSpec((parts, 1, rows, lanes), lambda o: (0, o, 0, 0)),
        out_shape=jax.ShapeDtypeStruct((parts, owners, rows, lanes), jnp.bfloat16),
        compiler_params=pltpu.CompilerParams(vmem_limit_bytes=32 << 20),
        name="pack_rows",
    )(grad_rows, slot_index)


def table_kernel(swapped, chunk_ref, ids_ref, out_ref, hold_ref):
    sources, rows, lanes = chunk_ref.shape
    block, columns = out_ref.shape
    slots = ids_ref.shape[1]
    capacity = slots // sources

    @pl.when(pl.program_id(0) == 0)
    def unpack():
        if lanes == columns:
            for source in range(sources):
                hold_ref[source * capacity : (source + 1) * capacity, :] = chunk_ref[source]
            return

        def one(source, carry):
            base = pl.multiple_of(source * capacity, capacity)
            full = columns // 128
            for tile in range(full):
                hold_ref[pl.ds(base, capacity), tile * 128 : (tile + 1) * 128] = chunk_ref[
                    source, tile * capacity : (tile + 1) * capacity, :
                ]
            mixed = chunk_ref[source, full * capacity :, :].astype(jnp.float32)
            turned = pltpu.roll(mixed, 64, 1).astype(jnp.bfloat16)
            half = capacity // 2
            hold_ref[pl.ds(base, half), full * 128 :] = mixed.astype(jnp.bfloat16)[:, :64]
            hold_ref[pl.ds(base + half, half), full * 128 :] = turned[:, :64]
            return carry

        lax.fori_loop(0, sources, one, 0)

    places = pl.program_id(0) * block + lax.broadcasted_iota(jnp.int32, (block, 512), 0)
    total = jnp.zeros((block, columns), jnp.float32)
    for start in range(0, slots, 512):
        hot = jnp.where(places == ids_ref[:, start : start + 512], 1.0, 0.0)
        total = total + product(hot.astype(jnp.bfloat16), hold_ref[start : start + 512, :])
    out_ref[...] = total


def add_rows(chunks, ids, table_rows, columns):
    sources, rows, lanes = chunks.shape
    slots = ids.shape[1]
    block = table_rows // 6 if table_rows % 48 == 0 else table_rows
    return pl.pallas_call(
        functools.partial(table_kernel, False),
        grid=(table_rows // block,),
        in_specs=[
            pl.BlockSpec((sources, rows, lanes), lambda b: (0, 0, 0)),
            pl.BlockSpec((1, slots), lambda b: (0, 0)),
        ],
        out_specs=pl.BlockSpec((block, columns), lambda b: (b, 0)),
        out_shape=jax.ShapeDtypeStruct((table_rows, columns), jnp.float32),
        scratch_shapes=[pltpu.VMEM((slots, columns), jnp.bfloat16)],
        compiler_params=pltpu.CompilerParams(vmem_limit_bytes=40 << 20),
        name="add_rows",
    )(chunks, ids)


def swap_half(blocks, axis, bit):
    size = lax.axis_size("emb")
    mine = (lax.axis_index("emb") >> bit) & 1
    keep = lax.dynamic_index_in_dim(blocks, mine, axis, keepdims=False)
    send = lax.dynamic_index_in_dim(blocks, 1 - mine, axis, keepdims=False)
    got = lax.ppermute(send, "emb", [(i, i ^ (1 << bit)) for i in range(size)])
    return (keep.astype(jnp.float32) + got.astype(jnp.float32)).astype(jnp.bfloat16)


def swap_all(blocks, order, held):
    for bit in order:
        blocks = swap_half(blocks, 1 + held.index(bit), bit)
        held = [other for other in held if other != bit]
    return blocks


def scatter_sum(array):
    owners = lax.axis_size("emb")
    groups = lax.axis_size("dp")
    bits = owners.bit_length() - 1
    rows, columns = array.shape
    share = rows // (owners * groups)
    blocks = array.reshape((groups,) + (2,) * bits + (share, columns))
    held = list(range(bits))[::-1]
    blocks = swap_half(blocks, 1 + held.index(0), 0)
    held.remove(0)
    cut = columns // 256 * 128
    upward = list(range(1, bits))
    parts = [
        swap_all(blocks[..., :cut], upward, held),
        swap_all(blocks[..., cut:], upward[::-1], held),
    ]
    parts = [lax.all_to_all(part, "dp", 0, 0, tiled=True) for part in parts]
    return jnp.concatenate([jnp.sum(part.astype(jnp.float32), 0) for part in parts], 1)


def columns_of(vectors):
    stacked = jnp.stack(vectors, 1).astype(jnp.bfloat16)
    return jnp.pad(stacked, ((0, 0), (0, 128 - len(vectors))))


def on_device(
    pixels,
    counts,
    token_ids,
    action_bins,
    patch_pos,
    token_table,
    pos_table,
    w_patch,
    w_res_a,
    w_res_b,
    gain_one,
    bias_one,
    w_q,
    w_k,
    w_v,
    w_o,
    gain_two,
    bias_two,
    w_up,
    w_down,
    cotangent,
):
    length = pixels.shape[0]
    model_width = w_q.shape[0]
    positions = jnp.arange(length)
    image_rows = positions < counts[0, 0]
    action_rows = positions >= length - counts[0, 1]
    table_rows = jnp.logical_not(image_rows)
    row_ids = jnp.where(action_rows, TEXT_VOCAB + action_bins, token_ids)
    rows_owned = token_table.shape[0]
    owners_total = lax.axis_size("emb")
    capacity = 3 * length // (2 * owners_total)
    owner_index = row_ids // rows_owned
    local_row = row_ids - owner_index * rows_owned
    owner_hot = (
        (owner_index[:, None] == jnp.arange(owners_total)[None, :]) & table_rows[:, None]
    ).astype(jnp.int32)
    earlier = jnp.cumsum(owner_hot, 0) - owner_hot
    rank_within = jnp.sum(earlier * owner_hot, 1)
    slot_index = jnp.where(
        table_rows, owner_index * capacity + rank_within, owners_total * capacity
    )
    request = (
        jnp.full((owners_total * capacity + 1,), -1, jnp.int32)
        .at[slot_index]
        .set(jnp.where(table_rows, local_row, -1))
    )
    received = lax.all_to_all(
        request[:-1].reshape(owners_total, capacity), "emb", split_axis=0, concat_axis=0, tiled=True
    )
    valid_slots = received >= 0
    local_ids = jnp.maximum(received, 0)
    fetched = jnp.where(valid_slots[..., None], token_table[local_ids], jnp.zeros((), jnp.bfloat16))
    returned = lax.all_to_all(fetched, "emb", split_axis=0, concat_axis=0, tiled=True)
    slot_safe = jnp.minimum(slot_index, owners_total * capacity - 1)
    table_embed = returned.reshape(owners_total * capacity, model_width)[slot_safe].astype(
        jnp.float32
    )
    patch_first = product(pixels, w_patch)
    first_low = patch_first.astype(jnp.bfloat16)
    res_inner = product(first_low, w_res_a)
    res_gelu, gelu_back_res = jax.vjp(jax.nn.gelu, res_inner)
    res_act = res_gelu.astype(jnp.bfloat16)
    res_mixed = product(res_act, w_res_b)
    position_hot = patch_pos[:, None] == jnp.arange(pos_table.shape[0])[None, :]
    position_embed = product(position_hot.astype(jnp.bfloat16), pos_table)
    image_embed = patch_first + res_mixed + position_embed
    embedded = jnp.where(image_rows[:, None], image_embed, table_embed)
    normed_one_f, norm_back_one = jax.vjp(
        norm_affine, embedded, gain_one.astype(jnp.float32), bias_one.astype(jnp.float32)
    )
    normed_one = normed_one_f.astype(jnp.bfloat16)
    queries = contract(w_q, normed_one, 0, 1).astype(jnp.bfloat16)
    key_heads = contract(w_k, normed_one, 0, 1).astype(jnp.bfloat16)
    value_heads = contract(w_v, normed_one, 0, 1).astype(jnp.bfloat16)
    attended, probs, inverse = attention_forward(queries, key_heads, value_heads)
    middle = embedded + product_left(attended, w_o)
    normed_two_f, norm_back_two = jax.vjp(
        norm_affine, middle, gain_two.astype(jnp.float32), bias_two.astype(jnp.float32)
    )
    normed_two = normed_two_f.astype(jnp.bfloat16)
    up_pre = product(normed_two, w_up)
    up_act, gelu_back_up = jax.vjp(jax.nn.gelu, up_pre)
    up_low = up_act.astype(jnp.bfloat16)
    output = (middle + product(up_low, w_down)).astype(jnp.bfloat16)
    grad_w_down = product_left(up_low, cotangent).astype(jnp.bfloat16)
    share_w_down = scatter_sum(grad_w_down)
    (grad_up_pre,) = gelu_back_up(product_right(cotangent, w_down))
    grad_up = grad_up_pre.astype(jnp.bfloat16)
    grad_w_up = product_left(normed_two, grad_up).astype(jnp.bfloat16)
    grad_normed_two = product_right(grad_up, w_up)
    grad_middle_norm, grad_gain_two, grad_bias_two = norm_back_two(grad_normed_two)
    grad_middle = cotangent.astype(jnp.float32) + grad_middle_norm
    grad_branch = grad_middle.astype(jnp.bfloat16)
    grad_w_o = product(attended, grad_branch).astype(jnp.bfloat16)
    share_up = scatter_sum(
        jnp.concatenate([grad_w_up, grad_w_o, columns_of([grad_gain_two, grad_bias_two])], 1)
    )
    grad_attended = product_right(w_o, grad_branch).astype(jnp.bfloat16)
    grad_heads = attention_backward(
        queries, key_heads, value_heads, attended, grad_attended, probs, inverse
    ).reshape(3 * model_width, length)
    grad_w_heads = contract(normed_one, grad_heads, 0, 1).astype(jnp.bfloat16)
    grad_normed_one = product_left(grad_heads, jnp.concatenate([w_q.T, w_k.T, w_v.T], 0))
    grad_embed_norm, grad_gain_one, grad_bias_one = norm_back_one(grad_normed_one)
    share_heads = scatter_sum(
        jnp.concatenate([grad_w_heads, columns_of([grad_gain_one, grad_bias_one])], 1)
    )
    grad_embedded = grad_middle + grad_embed_norm
    grad_low = grad_embedded.astype(jnp.bfloat16)
    groups = lax.axis_size("dp")
    columns = model_width // groups
    all_ids = lax.all_gather(received, "dp", axis=0, tiled=False).reshape(1, -1)
    chunks = pack_rows(grad_low, slot_index.reshape(1, length), groups, owners_total, capacity)
    chunks = lax.all_to_all(
        chunks.reshape((groups * owners_total,) + chunks.shape[2:]), BOTH, 0, 0, tiled=True
    )
    grad_table = add_rows(chunks, all_ids, rows_owned, columns)
    grad_image = jnp.where(image_rows[:, None], grad_embedded, 0.0)
    grad_mixed = grad_image.astype(jnp.bfloat16)
    grad_pos_table = product_left(position_hot.astype(jnp.bfloat16), grad_mixed)
    grad_w_res_b = product_left(res_act, grad_mixed).astype(jnp.bfloat16)
    (grad_inner_f,) = gelu_back_res(product_right(grad_mixed, w_res_b))
    grad_inner = grad_inner_f.astype(jnp.bfloat16)
    grad_w_res_a = product_left(first_low, grad_inner).astype(jnp.bfloat16)
    grad_first = (grad_image + product_right(grad_inner, w_res_a)).astype(jnp.bfloat16)
    grad_w_patch = product_left(pixels, grad_first).astype(jnp.bfloat16)
    grad_pixels = product_right(grad_first, w_patch)
    devices = groups * owners_total
    pos_rows = pos_table.shape[0]
    share = model_width // devices
    pos_columns = pos_rows * model_width // model_width
    spread = grad_pos_table.astype(jnp.bfloat16).reshape(model_width, pos_columns)
    share_res = scatter_sum(
        jnp.concatenate([grad_w_patch, grad_w_res_a, grad_w_res_b, spread], 1)
    )
    wide = w_up.shape[1]

    def cut(array, place):
        return array[:, place * model_width : (place + 1) * model_width]

    return (
        output,
        grad_pixels,
        grad_table,
        share_res[:, 3 * model_width :].reshape(pos_rows // devices, model_width),
        cut(share_res, 0),
        cut(share_res, 1),
        cut(share_res, 2),
        share_heads[:, 3 * model_width],
        share_heads[:, 3 * model_width + 1],
        cut(share_heads, 0),
        cut(share_heads, 1),
        cut(share_heads, 2),
        share_up[:, wide : wide + model_width],
        share_up[:, wide + model_width],
        share_up[:, wide + model_width + 1],
        share_up[:, :wide],
        share_w_down,
    )


def solution(mesh):
    in_specs = (
        P(("dp", "emb"), None),
        P(("dp", "emb"), None),
        P(("dp", "emb")),
        P(("dp", "emb")),
        P(("dp", "emb")),
        P("emb", None),
        P(),
        P(),
        P(),
        P(),
        P(),
        P(),
        P(),
        P(),
        P(),
        P(),
        P(),
        P(),
        P(),
        P(),
        P(("dp", "emb"), None),
    )
    out_specs = (
        P(("dp", "emb"), None),
        P(("dp", "emb"), None),
        P("emb", "dp"),
        P(("dp", "emb"), None),
        P(("dp", "emb"), None),
        P(("dp", "emb"), None),
        P(("dp", "emb"), None),
        P(("dp", "emb")),
        P(("dp", "emb")),
        P(("dp", "emb"), None),
        P(("dp", "emb"), None),
        P(("dp", "emb"), None),
        P(("dp", "emb"), None),
        P(("dp", "emb")),
        P(("dp", "emb")),
        P(("dp", "emb"), None),
        P(("dp", "emb"), None),
    )
    return jax.shard_map(
        on_device, mesh=mesh, in_specs=in_specs, out_specs=out_specs, check_vma=False
    )
```

time: 1510 us -> 527 us (0.35)
  the two profiles are of different devices: /device:TPU:1 before, /device:TPU:0 now
where the time goes in v1:
time: 527 us; the launch traced here: 518 us
  matrix products  120 us (23%)
  Pallas kernels  116 us (22%)
  waiting for transfers between devices  73.1 us (14%)
  local copies, waits for them, and re-layouts  70.9 us (13%)
  starting transfers between devices  58.2 us (11%)
  other arithmetic  53.3 us (10%)
  blocking collectives  23.2 us (4%)
    dot_general x25, matrix products, contract(): lax.dot_general(left, right, (((left_dim,), (right_dim,)), ((), ())), pre...  120 us
    ppermute x20, waiting for transfers between devices, swap_half(): got = lax.ppermute(send, 'emb', [(i, i ^ 1 << bit) for i in range(size)])  51.2 us
    pallas_call x1, Pallas kernels, attention_backward(): pl.pallas_call(functools.partial(backward_kernel, HEADS_STEP), grid=(head...  47.4 us
    pallas_call x1, Pallas kernels, attention_forward(): pl.pallas_call(functools.partial(forward_kernel, HEADS_STEP), grid=(heads...  45.3 us
    all_to_all x8, starting transfers between devices, scatter_sum(): parts = [lax.all_to_all(part, 'dp', 0, 0, tiled=True) for part in parts]  33.3 us
    convert_element_type x20, other arithmetic, swap_half(): (keep.astype(jnp.float32) + got.astype(jnp.float32)).astype(jnp.bfloat16)  25.7 us
    unnamed x167, local copies, waits for them, and re-layouts  22.7 us
    all_to_all x8, waiting for transfers between devices, scatter_sum(): parts = [lax.all_to_all(part, 'dp', 0, 0, tiled=True) for part in parts]  20.8 us
  transfers between devices with their start and end apart: 30, of which 13 were waited for; matrix products, arithmetic and copies ran while one was open for 20% of the time, Pallas kernels for 4%

profile of v1, /device:TPU:0, one launch (start us, length us, event | category | flops | bytes accessed | tf_op | source)
XLA Modules:
  0.0 518.2 jit_solution(6445217391510486055)
XLA Ops:
  13.9 9.7 %all_to_all.59 = s32[8,1,192]{2,1,0:T(1,128)S(1)} all-to-all(s32[8,1,192]{2,1,0:T(1,128)S(1)} %all_to_all.36), channel_id=1, replica_groups=mesh['dp'=4,'emb'=8] {'emb'}, dimensions={0} | all-to-all | bytes 12288 | tf_op jit(solution)/shard_map/all_to_all | solution.py:387
  23.6 10.3 %gather_fusion = bf16[1536,768]{1,0:T(8,128)(2,1)} fusion(bf16[4128,768]{1,0:T(8,128)(2,1)} %param.26, s32[2048]{0:T(1024)S(1)} %pad_clamp_fusion), kind=kCustom, calls=%fused_computation | custom fusion | bytes 4724736 | tf_op jit(solution)/shard_map/gather | solution.py:392
  37.4 4.5 all-to-all-start.1
  56.6 13.5 %all-gather = s32[32,1,192]{2,1,0:T(1,128)S(1)} all-gather(s32[8,1,192]{2,1,0:T(1,128)S(1)} %all_to_all.59), channel_id=2, replica_groups=mesh['dp'=4,'emb'=8] {'dp'}, dimensions={0}, use_global_device_ids=true | all-gather | bytes 30720 | tf_op jit(solution)/shard_map/all_gather | solution.py:452
  71.4 6.5 %gather_fusion.1 = bf16[1024,768]{1,0:T(8,128)(2,1)S(1)} fusion(bf16[1536,768]{1,0:T(8,128)(2,1)} %bitcast.6, s32[1024]{0:T(1024)S(1)} %get-tuple-element.124), kind=kCustom, calls=%fused_computation.1 | custom fusion | bytes 3149824 | tf_op jit(solution)/shard_map/gather | solution.py:395
  88.3 45.3 %attention_forward.1 = (bf16[768,1024]{1,0:T(8,128)(2,1)S(1)}, bf16[24,2560,256]{2,1,0:T(8,128)(2,1)}, f32[24,1,1024]{2,1,0:T(1,128)S(1)}) custom-call(bf16[768,1024]{1,0:T(8,128)(2,1)S(1)} %fusion.30.q_ref, bf16[768,1024]{1,0:T(8,128)(2,1)S(1)} %fusion.31.k_ref, bf16[768,1024]{1,0:T(8,128)(2,1)S(1)} %fusion.32.v_ref), custom_call_target="tpu_custom_call" | custom-call | flops 49999998976 | bytes 31457280 | tf_op jit(solution)/shard_map/attention_forward/pallas_call | solution.py:90
  137.5 8.4 %fusion.70 = f32[1024,3072]{1,0:T(8,128)} fusion(bf16[768,3072]{1,0:T(8,128)(2,1)S(1)} %bitcast.215, f32[1024,768]{1,0:T(8,128)S(1)} %get-tuple-element.143, f32[768]{0:T(1024)S(1)} %convert_element_type.394, f32[768]{0:T(1024)S(1)} %convert_element_type.393, f32[1024]{0:T(1024)S(1)} %fusion.66, f32[1024]{0:T(1024)S(1)} %broadcast_multiply_fusion), kind=kOutput, calls=%fused_computation.198 | convolution fusion | flops 4835770368 | bytes 20461568 | tf_op jit(solution)/shard_map/dot_general | solution.py:30
  145.9 11.6 %convolution_convert_fusion = bf16[3072,768]{1,0:T(8,128)(2,1)} fusion(bf16[1024,768]{1,0:T(8,128)(2,1)S(1)} %copy-done.12, f32[1024,3072]{1,0:T(8,128)} %fusion.70), kind=kOutput, calls=%fused_computation.20 | convolution fusion | flops 4862509056 | bytes 18874368 | tf_op jit(solution)/shard_map/dot_general | solution.py:30
  157.5 15.0 %fusion.6 = bf16[1024,3072]{1,0:T(8,128)(2,1)} fusion(f32[1024,3072]{1,0:T(8,128)} %fusion.70, bf16[1024,768]{1,0:T(8,128)(2,1)S(1)} %copy-done.12, bf16[3072,768]{1,0:T(8,128)(2,1)} %param.40), kind=kOutput, calls=%fused_computation.11 | convolution fusion | flops 4894752768 | bytes 25165824 | tf_op jit(solution)/shard_map/dot_general | solution.py:30
  172.5 9.1 %multiply_reduce_fusion = (bf16[768]{0:T(1024)(128)(2,1)S(1)}, f32[1024]{0:T(1024)S(1)}, bf16[768]{0:T(1024)(128)(2,1)S(1)}, f32[1024,768]{1,0:T(8,128)S(1)}) fusion(f32[1024,768]{1,0:T(8,128)S(1)} %get-tuple-element.143, f32[1024]{0:T(1024)S(1)} %fusion.66, f32[1024]{0:T(1024)S(1)} %broadcast_multiply_fusion, f32[768]{0:T(1024)S(1)} %convert_element_type.393, ...), kind=kOutput, calls=%fused_computation.48 | convolution fusion | flops 4838126592 | bytes 17319936 | tf_op jit(solution)/shard_map/dot_general | solution.py:30
  185.5 47.4 %attention_backward.1 = bf16[3,768,1024]{2,1,0:T(8,128)(2,1)S(1)} custom-call(bf16[768,1024]{1,0:T(8,128)(2,1)S(1)} %fusion.30.q_ref, bf16[768,1024]{1,0:T(8,128)(2,1)S(1)} %fusion.31.k_ref, bf16[768,1024]{1,0:T(8,128)(2,1)S(1)} %fusion.32.v_ref, bf16[768,1024]{1,0:T(8,128)(2,1)S(1)} %get-tuple-element.20.o_ref, bf16[768,1024]{1,0:T(8,128)(2,1)S(1)} %fusion.33.g_ref, ...), custom_call_target="tpu_custom_call" | custom-call | flops 54999998464 | bytes 31457280 | tf_op jit(solution)/shard_map/attention_backward/pallas_call | solution.py:158
  233.0 5.4 %convolution_convert_fusion.2 = bf16[768,2304]{1,0:T(8,128)(2,1)} fusion(bf16[1024,768]{1,0:T(8,128)(2,1)S(1)} %copy-done.25, bf16[2304,1024]{1,0:T(8,128)(2,1)S(1)} %bitcast.193), kind=kOutput, calls=%fused_computation.22 | convolution fusion | flops 3625648128 | bytes 9830400 | tf_op jit(solution)/shard_map/dot_general | solution.py:30
  238.5 4.8 multiply_reduce_fusion.1
  273.6 8.0 %convolution_convert_fusion.1 = bf16[768,3072]{1,0:T(8,128)(2,1)} fusion(bf16[1024,3072]{1,0:T(8,128)(2,1)S(1)} %bitcast.220, f32[1024,768]{1,0:T(8,128)S(1)} %copy-done.11, f32[768]{0:T(1024)S(1)} %copy-done.52, f32[768]{0:T(1024)S(1)} %convert_element_type.393, f32[1024]{0:T(1024)S(1)} %fusion.66, f32[1024]{0:T(1024)S(1)} %broadcast_multiply_fusion), kind=kOutput, calls=%fused_computation.21 | convolution fusion | flops 4838129664 | bytes 14170112 | tf_op jit(solution)/shard_map/dot_general | solution.py:30
  284.1 4.4 convolution_convert_fusion.7
  297.7 6.1 %collective-permute-done.8 = bf16[4,2,24,1152]{3,2,1,0:T(8,128)(2,1)S(1)} collective-permute-done((bf16[4,2,24,1152]{3,2,1,0:T(8,128)(2,1)S(1)}, bf16[4,2,24,1152]{3,2,1,0:T(8,128)(2,1)S(1)}, u32[]{:S(2)}, u32[]{:S(2)}) %collective-permute-start.8) | collective-permute-done | bytes 442400 | tf_op jit(solution)/shard_map/ppermute | solution.py:303
  323.3 4.6 all-to-all-start.6
  329.8 7.4 %collective-permute-done.2 = bf16[4,24,1280]{2,1,0:T(8,128)(2,1)} collective-permute-done((bf16[4,24,1280]{2,1,0:T(8,128)(2,1)}, bf16[4,24,1280]{2,1,0:T(8,128)(2,1)}, u32[]{:S(2)}, u32[]{:S(2)}) %collective-permute-start.2) | collective-permute-done | bytes 245792 | tf_op jit(solution)/shard_map/ppermute | solution.py:303
  339.7 4.8 all-to-all-start.5
  346.4 6.2 %all-to-all-done.5 = bf16[4,24,1280]{2,1,0:T(8,128)(2,1)S(1)} async-done(((bf16[4,24,1280]{2,1,0:T(8,128)(2,1)}), bf16[4,24,1280]{2,1,0:T(8,128)(2,1)S(1)}, u32[]{:S(2)}, u32[]{:S(2)}) %all-to-all-start.5) | async-done | bytes 245792 | tf_op jit(solution)/shard_map/all_to_all | solution.py:330
  378.2 6.4 %fusion.9 = bf16[768,3968]{1,0:T(8,128)(2,1)} fusion(bf16[768,2]{1,0:T(8,128)(2,1)} %copy.100, bf16[768,768]{1,0:T(8,128)(2,1)} %convolution_convert_fusion.7, bf16[768,3072]{1,0:T(8,128)(2,1)} %convolution_convert_fusion.1), kind=kLoop, calls=%fused_computation.17 | loop fusion | flops 24379392 | bytes 11996160 | tf_op jit(solution)/shard_map/concatenate | solution.py:436
  386.3 5.0 all-to-all-start.9
  395.1 4.7 pack_rows.1
  401.2 6.0 %all-to-all-start.2 = ((bf16[32,288,128]{2,1,0:T(8,128)(2,1)}), bf16[32,288,128]{2,1,0:T(8,128)(2,1)}, u32[]{:S(2)}, u32[]{:S(2)}) async-start(bf16[32,288,128]{2,1,0:T(8,128)(2,1)} %bitcast.191), calls=%async_computation.2 | async-start | bytes 4718592 | tf_op jit(solution)/shard_map/all_to_all | solution.py:454
  407.3 13.1 %add_convert_fusion.1 = bf16[1024,768]{1,0:T(8,128)(2,1)} fusion(f32[1024,768]{1,0:T(8,128)} %copy-done.10, bf16[3072,768]{1,0:T(8,128)(2,1)} %param.40, f32[1024,3072]{1,0:T(8,128)} %fusion.70), kind=kOutput, calls=%fused_computation.55 | convolution fusion | flops 4861722624 | bytes 22020096 | tf_op jit(solution)/shard_map/dot_general | solution.py:30
  431.7 21.2 %collective-permute-done.13 = bf16[4,2,24,1920]{3,2,1,0:T(8,128)(2,1)S(1)} collective-permute-done((bf16[4,2,24,1920]{3,2,1,0:T(8,128)(2,1)S(1)}, bf16[4,2,24,1920]{3,2,1,0:T(8,128)(2,1)S(1)}, u32[]{:S(2)}, u32[]{:S(2)}) %collective-permute-start.13) | collective-permute-done | bytes 737312 | tf_op jit(solution)/shard_map/ppermute | solution.py:303
  453.2 5.8 %collective-permute-done.11 = bf16[4,2,24,2048]{3,2,1,0:T(8,128)(2,1)S(1)} collective-permute-done((bf16[4,2,24,2048]{3,2,1,0:T(8,128)(2,1)S(1)}, bf16[4,2,24,2048]{3,2,1,0:T(8,128)(2,1)S(1)}, u32[]{:S(2)}, u32[]{:S(2)}) %collective-permute-start.11) | collective-permute-done | bytes 786464 | tf_op jit(solution)/shard_map/ppermute | solution.py:303
  460.1 6.2 %collective-permute-done.14 = bf16[4,24,1920]{2,1,0:T(8,128)(2,1)S(1)} collective-permute-done((bf16[4,24,1920]{2,1,0:T(8,128)(2,1)S(1)}, bf16[4,24,1920]{2,1,0:T(8,128)(2,1)S(1)}, u32[]{:S(2)}, u32[]{:S(2)}) %collective-permute-start.14) | collective-permute-done | bytes 368672 | tf_op jit(solution)/shard_map/ppermute | solution.py:303
  467.1 5.1 all-to-all-start.8
  474.0 9.2 %all-to-all-done.8 = bf16[4,24,1920]{2,1,0:T(8,128)(2,1)S(1)} async-done(((bf16[4,24,1920]{2,1,0:T(8,128)(2,1)}), bf16[4,24,1920]{2,1,0:T(8,128)(2,1)S(1)}, u32[]{:S(2)}, u32[]{:S(2)}) %all-to-all-start.8) | async-done | bytes 368672 | tf_op jit(solution)/shard_map/all_to_all | solution.py:330
  489.8 18.4 %add_rows.1 = f32[4128,192]{1,0:T(8,128)S(1)} custom-call(bf16[32,288,128]{2,1,0:T(8,128)(2,1)} %all-to-all-done.2.chunk_ref, s32[1,6144]{1,0:T(1,128)S(1)} %reshape.237.ids_ref), custom_call_target="tpu_custom_call" | custom-call | tf_op jit(solution)/shard_map/add_rows/pallas_call | solution.py:283
  510.2 5.3 %copy.101 = f32[4128,192]{0,1:T(8,128)} copy(f32[4128,192]{1,0:T(8,128)} %copy-done.1) | data formatting | bytes 6340608
  (351 shorter events, 175.4 us)
Async XLA Ops:
  37.4 34.0 %all-to-all-start.1 = ((bf16[8,192,768]{2,1,0:T(8,128)(2,1)}), bf16[8,192,768]{2,1,0:T(8,128)(2,1)}, u32[]{:S(2)}, u32[]{:S(2)}) async-start(bf16[8,192,768]{2,1,0:T(8,128)(2,1)} %broadcast_select_fusion), calls=%async_computation.1 | async-start | bytes 4718592 | tf_op jit(solution)/shard_map/all_to_all | solution.py:393
  42.0 93.8 %copy-start.51 = (f32[768]{0:T(1024)}, f32[768]{0:T(1024)S(1)}, u32[]{:S(2)}) copy-start(f32[768]{0:T(1024)S(1)} %convert_element_type.394) | copy-start | bytes 9220
  133.7 51.8 %copy-start.5 = (bf16[768,1024]{1,0:T(8,128)(2,1)}, bf16[768,1024]{1,0:T(8,128)(2,1)S(1)}, u32[]{:S(2)}) copy-start(bf16[768,1024]{1,0:T(8,128)(2,1)S(1)} %get-tuple-element.20.o_ref) | copy-start | bytes 4718596
  266.3 22.3 %collective-permute-start.5 = (bf16[4,2,2,24,2432]{4,3,2,1,0:T(8,128)(2,1)}, bf16[4,2,2,24,2432]{4,3,2,1,0:T(8,128)(2,1)}, u32[]{:S(2)}, u32[]{:S(2)}) collective-permute-start(bf16[4,2,2,24,2432]{4,3,2,1,0:T(8,128)(2,1)} %dynamic-slice_bitcast_fusion.3), channel_id=1, source_target_pairs={{0,1},{1,0},{2,3},{3,2},{4,5},{5,4},{6,7},{7,6},{8,9},{9,8},{10,11... | collective-permute-start | bytes 5603336 | tf_op jit(solution)/shard_map/ppermute | solution.py:303
  272.4 20.8 %collective-permute-start = (bf16[4,2,2,24,2560]{4,3,2,1,0:T(8,128)(2,1)}, bf16[4,2,2,24,2560]{4,3,2,1,0:T(8,128)(2,1)}, u32[]{:S(2)}, u32[]{:S(2)}) collective-permute-start(bf16[4,2,2,24,2560]{4,3,2,1,0:T(8,128)(2,1)} %dynamic-slice_bitcast_fusion.2), channel_id=1, source_target_pairs={{0,1},{1,0},{2,3},{3,2},{4,5},{5,4},{6,7},{7,6},{8,9},{9,8},{10,11... | collective-permute-start | bytes 5898248 | tf_op jit(solution)/shard_map/ppermute | solution.py:303
  283.2 24.7 %collective-permute-start.15 = (bf16[4,2,2,96,768]{4,3,2,1,0:T(8,128)(2,1)}, bf16[4,2,2,96,768]{4,3,2,1,0:T(8,128)(2,1)}, u32[]{:S(2)}, u32[]{:S(2)}) collective-permute-start(bf16[4,2,2,96,768]{4,3,2,1,0:T(8,128)(2,1)} %dynamic-slice_bitcast_fusion.1), channel_id=1, source_target_pairs={{0,1},{1,0},{2,3},{3,2},{4,5},{5,4},{6,7},{7,6},{8,9},{9,8},{10,11... | collective-permute-start | bytes 7077896 | tf_op jit(solution)/shard_map/ppermute | solution.py:303
  290.8 13.0 %collective-permute-start.8 = (bf16[4,2,24,1152]{3,2,1,0:T(8,128)(2,1)S(1)}, bf16[4,2,24,1152]{3,2,1,0:T(8,128)(2,1)S(1)}, u32[]{:S(2)}, u32[]{:S(2)}) collective-permute-start(bf16[4,2,24,1152]{3,2,1,0:T(8,128)(2,1)S(1)} %dynamic-slice_bitcast_fusion.11), channel_id=1, source_target_pairs={{0,2},{1,3},{2,0},{3,1},{4,6},{5,7},{6,4},{7,5},{8,10},{9,11},{10,... | collective-permute-start | bytes 1327112 | tf_op jit(solution)/shard_map/ppermute | solution.py:303
  291.7 14.1 %collective-permute-start.6 = (bf16[4,2,24,1280]{3,2,1,0:T(8,128)(2,1)S(1)}, bf16[4,2,24,1280]{3,2,1,0:T(8,128)(2,1)S(1)}, u32[]{:S(2)}, u32[]{:S(2)}) collective-permute-start(bf16[4,2,24,1280]{3,2,1,0:T(8,128)(2,1)S(1)} %dynamic-slice_bitcast_fusion.8), channel_id=1, source_target_pairs={{0,4},{1,5},{2,6},{3,7},{4,0},{5,1},{6,2},{7,3},{8,12},{9,13},{10,... | collective-permute-start | bytes 1474568 | tf_op jit(solution)/shard_map/ppermute | solution.py:303
  295.8 20.6 %collective-permute-start.1 = (bf16[4,2,24,1280]{3,2,1,0:T(8,128)(2,1)S(1)}, bf16[4,2,24,1280]{3,2,1,0:T(8,128)(2,1)S(1)}, u32[]{:S(2)}, u32[]{:S(2)}) collective-permute-start(bf16[4,2,24,1280]{3,2,1,0:T(8,128)(2,1)S(1)} %dynamic-slice_bitcast_fusion.10), channel_id=1, source_target_pairs={{0,4},{1,5},{2,6},{3,7},{4,0},{5,1},{6,2},{7,3},{8,12},{9,13},{10,... | collective-permute-start | bytes 1474568 | tf_op jit(solution)/shard_map/ppermute | solution.py:303
  296.4 22.1 %collective-permute-start.3 = (bf16[4,2,24,1280]{3,2,1,0:T(8,128)(2,1)S(1)}, bf16[4,2,24,1280]{3,2,1,0:T(8,128)(2,1)S(1)}, u32[]{:S(2)}, u32[]{:S(2)}) collective-permute-start(bf16[4,2,24,1280]{3,2,1,0:T(8,128)(2,1)S(1)} %dynamic-slice_bitcast_fusion.9), channel_id=1, source_target_pairs={{0,2},{1,3},{2,0},{3,1},{4,6},{5,7},{6,4},{7,5},{8,10},{9,11},{10,... | collective-permute-start | bytes 1474568 | tf_op jit(solution)/shard_map/ppermute | solution.py:303
  304.0 17.1 %collective-permute-start.9 = (bf16[4,24,1152]{2,1,0:T(8,128)(2,1)S(1)}, bf16[4,24,1152]{2,1,0:T(8,128)(2,1)S(1)}, u32[]{:S(2)}, u32[]{:S(2)}) collective-permute-start(bf16[4,24,1152]{2,1,0:T(8,128)(2,1)S(1)} %dynamic-slice_bitcast_fusion.19), channel_id=1, source_target_pairs={{0,4},{1,5},{2,6},{3,7},{4,0},{5,1},{6,2},{7,3},{8,12},{9,13},{10,... | collective-permute-start | bytes 663560 | tf_op jit(solution)/shard_map/ppermute | solution.py:303
  306.7 21.2 %collective-permute-start.7 = (bf16[4,24,1280]{2,1,0:T(8,128)(2,1)}, bf16[4,24,1280]{2,1,0:T(8,128)(2,1)}, u32[]{:S(2)}, u32[]{:S(2)}) collective-permute-start(bf16[4,24,1280]{2,1,0:T(8,128)(2,1)} %dynamic-slice_bitcast_fusion.16), channel_id=1, source_target_pairs={{0,2},{1,3},{2,0},{3,1},{4,6},{5,7},{6,4},{7,5},{8,10},{9,11},{10,... | collective-permute-start | bytes 737288 | tf_op jit(solution)/shard_map/ppermute | solution.py:303
  311.8 44.8 %collective-permute-start.18 = (bf16[4,2,96,384]{3,2,1,0:T(8,128)(2,1)}, bf16[4,2,96,384]{3,2,1,0:T(8,128)(2,1)}, u32[]{:S(2)}, u32[]{:S(2)}) collective-permute-start(bf16[4,2,96,384]{3,2,1,0:T(8,128)(2,1)} %dynamic-slice_bitcast_fusion.6), channel_id=1, source_target_pairs={{0,4},{1,5},{2,6},{3,7},{4,0},{5,1},{6,2},{7,3},{8,12},{9,13},{10,... | collective-permute-start | bytes 1769480 | tf_op jit(solution)/shard_map/ppermute | solution.py:303
  316.4 51.1 %collective-permute-start.16 = (bf16[4,2,96,384]{3,2,1,0:T(8,128)(2,1)}, bf16[4,2,96,384]{3,2,1,0:T(8,128)(2,1)}, u32[]{:S(2)}, u32[]{:S(2)}) collective-permute-start(bf16[4,2,96,384]{3,2,1,0:T(8,128)(2,1)} %dynamic-slice_bitcast_fusion.7), channel_id=1, source_target_pairs={{0,2},{1,3},{2,0},{3,1},{4,6},{5,7},{6,4},{7,5},{8,10},{9,11},{10,... | collective-permute-start | bytes 1769480 | tf_op jit(solution)/shard_map/ppermute | solution.py:303
  318.6 18.6 %collective-permute-start.2 = (bf16[4,24,1280]{2,1,0:T(8,128)(2,1)}, bf16[4,24,1280]{2,1,0:T(8,128)(2,1)}, u32[]{:S(2)}, u32[]{:S(2)}) collective-permute-start(bf16[4,24,1280]{2,1,0:T(8,128)(2,1)} %dynamic-slice_bitcast_fusion.18), channel_id=1, source_target_pairs={{0,2},{1,3},{2,0},{3,1},{4,6},{5,7},{6,4},{7,5},{8,10},{9,11},{10,... | collective-permute-start | bytes 737288 | tf_op jit(solution)/shard_map/ppermute | solution.py:303
  321.1 23.5 %collective-permute-start.4 = (bf16[4,24,1280]{2,1,0:T(8,128)(2,1)}, bf16[4,24,1280]{2,1,0:T(8,128)(2,1)}, u32[]{:S(2)}, u32[]{:S(2)}) collective-permute-start(bf16[4,24,1280]{2,1,0:T(8,128)(2,1)} %dynamic-slice_bitcast_fusion.17), channel_id=1, source_target_pairs={{0,4},{1,5},{2,6},{3,7},{4,0},{5,1},{6,2},{7,3},{8,12},{9,13},{10,... | collective-permute-start | bytes 737288 | tf_op jit(solution)/shard_map/ppermute | solution.py:303
  323.3 15.7 %all-to-all-start.6 = ((bf16[4,24,1152]{2,1,0:T(8,128)(2,1)}), bf16[4,24,1152]{2,1,0:T(8,128)(2,1)S(1)}, u32[]{:S(2)}, u32[]{:S(2)}) async-start(bf16[4,24,1152]{2,1,0:T(8,128)(2,1)} %fusion.53), calls=%async_computation.6 | async-start | bytes 442368 | tf_op jit(solution)/shard_map/all_to_all | solution.py:330
  339.7 12.9 %all-to-all-start.5 = ((bf16[4,24,1280]{2,1,0:T(8,128)(2,1)}), bf16[4,24,1280]{2,1,0:T(8,128)(2,1)S(1)}, u32[]{:S(2)}, u32[]{:S(2)}) async-start(bf16[4,24,1280]{2,1,0:T(8,128)(2,1)} %fusion.50), calls=%async_computation.5 | async-start | bytes 491520 | tf_op jit(solution)/shard_map/all_to_all | solution.py:330
  353.2 10.1 %all-to-all-start.3 = ((bf16[4,24,1280]{2,1,0:T(8,128)(2,1)}), bf16[4,24,1280]{2,1,0:T(8,128)(2,1)S(1)}, u32[]{:S(2)}, u32[]{:S(2)}) async-start(bf16[4,24,1280]{2,1,0:T(8,128)(2,1)} %fusion.52), calls=%async_computation.3 | async-start | bytes 491520 | tf_op jit(solution)/shard_map/all_to_all | solution.py:330
  359.6 10.8 %collective-permute-start.19 = (bf16[4,96,384]{2,1,0:T(8,128)(2,1)}, bf16[4,96,384]{2,1,0:T(8,128)(2,1)}, u32[]{:S(2)}, u32[]{:S(2)}) collective-permute-start(bf16[4,96,384]{2,1,0:T(8,128)(2,1)} %dynamic-slice_bitcast_fusion.14), channel_id=1, source_target_pairs={{0,2},{1,3},{2,0},{3,1},{4,6},{5,7},{6,4},{7,5},{8,10},{9,11},{10,... | collective-permute-start | bytes 884744 | tf_op jit(solution)/shard_map/ppermute | solution.py:303
  364.0 10.0 %all-to-all-start.4 = ((bf16[4,24,1280]{2,1,0:T(8,128)(2,1)}), bf16[4,24,1280]{2,1,0:T(8,128)(2,1)S(1)}, u32[]{:S(2)}, u32[]{:S(2)}) async-start(bf16[4,24,1280]{2,1,0:T(8,128)(2,1)} %fusion.51), calls=%async_computation.4 | async-start | bytes 491520 | tf_op jit(solution)/shard_map/all_to_all | solution.py:330
  370.4 14.2 %collective-permute-start.17 = (bf16[4,96,384]{2,1,0:T(8,128)(2,1)}, bf16[4,96,384]{2,1,0:T(8,128)(2,1)}, u32[]{:S(2)}, u32[]{:S(2)}) collective-permute-start(bf16[4,96,384]{2,1,0:T(8,128)(2,1)} %dynamic-slice_bitcast_fusion.15), channel_id=1, source_target_pairs={{0,4},{1,5},{2,6},{3,7},{4,0},{5,1},{6,2},{7,3},{8,12},{9,13},{10,... | collective-permute-start | bytes 884744 | tf_op jit(solution)/shard_map/ppermute | solution.py:303
  374.7 11.6 %all-to-all-start.10 = ((bf16[4,96,384]{2,1,0:T(8,128)(2,1)}), bf16[4,96,384]{2,1,0:T(8,128)(2,1)S(1)}, u32[]{:S(2)}, u32[]{:S(2)}) async-start(bf16[4,96,384]{2,1,0:T(8,128)(2,1)} %fusion.46), calls=%async_computation.10 | async-start | bytes 589824 | tf_op jit(solution)/shard_map/all_to_all | solution.py:330
  386.3 14.9 %all-to-all-start.9 = ((bf16[4,96,384]{2,1,0:T(8,128)(2,1)}), bf16[4,96,384]{2,1,0:T(8,128)(2,1)}, u32[]{:S(2)}, u32[]{:S(2)}) async-start(bf16[4,96,384]{2,1,0:T(8,128)(2,1)} %fusion.47), calls=%async_computation.9 | async-start | bytes 589824 | tf_op jit(solution)/shard_map/all_to_all | solution.py:330
  395.1 28.4 %collective-permute-start.10 = (bf16[4,2,2,24,3968]{4,3,2,1,0:T(8,128)(2,1)}, bf16[4,2,2,24,3968]{4,3,2,1,0:T(8,128)(2,1)}, u32[]{:S(2)}, u32[]{:S(2)}) collective-permute-start(bf16[4,2,2,24,3968]{4,3,2,1,0:T(8,128)(2,1)} %dynamic-slice_bitcast_fusion), channel_id=1, source_target_pairs={{0,1},{1,0},{2,3},{3,2},{4,5},{5,4},{6,7},{7,6},{8,9},{9,8},{10,11... | collective-permute-start | bytes 9142280 | tf_op jit(solution)/shard_map/ppermute | solution.py:303
  401.2 65.8 %all-to-all-start.2 = ((bf16[32,288,128]{2,1,0:T(8,128)(2,1)}), bf16[32,288,128]{2,1,0:T(8,128)(2,1)}, u32[]{:S(2)}, u32[]{:S(2)}) async-start(bf16[32,288,128]{2,1,0:T(8,128)(2,1)} %bitcast.191), calls=%async_computation.2 | async-start | bytes 4718592 | tf_op jit(solution)/shard_map/all_to_all | solution.py:454
  426.5 26.4 %collective-permute-start.13 = (bf16[4,2,24,1920]{3,2,1,0:T(8,128)(2,1)S(1)}, bf16[4,2,24,1920]{3,2,1,0:T(8,128)(2,1)S(1)}, u32[]{:S(2)}, u32[]{:S(2)}) collective-permute-start(bf16[4,2,24,1920]{3,2,1,0:T(8,128)(2,1)S(1)} %dynamic-slice_bitcast_fusion.5), channel_id=1, source_target_pairs={{0,2},{1,3},{2,0},{3,1},{4,6},{5,7},{6,4},{7,5},{8,10},{9,11},{10,... | collective-permute-start | bytes 2211848 | tf_op jit(solution)/shard_map/ppermute | solution.py:303
  430.1 28.9 %collective-permute-start.11 = (bf16[4,2,24,2048]{3,2,1,0:T(8,128)(2,1)S(1)}, bf16[4,2,24,2048]{3,2,1,0:T(8,128)(2,1)S(1)}, u32[]{:S(2)}, u32[]{:S(2)}) collective-permute-start(bf16[4,2,24,2048]{3,2,1,0:T(8,128)(2,1)S(1)} %dynamic-slice_bitcast_fusion.4), channel_id=1, source_target_pairs={{0,4},{1,5},{2,6},{3,7},{4,0},{5,1},{6,2},{7,3},{8,12},{9,13},{10,... | collective-permute-start | bytes 2359304 | tf_op jit(solution)/shard_map/ppermute | solution.py:303
  453.1 13.1 %collective-permute-start.14 = (bf16[4,24,1920]{2,1,0:T(8,128)(2,1)S(1)}, bf16[4,24,1920]{2,1,0:T(8,128)(2,1)S(1)}, u32[]{:S(2)}, u32[]{:S(2)}) collective-permute-start(bf16[4,24,1920]{2,1,0:T(8,128)(2,1)S(1)} %dynamic-slice_bitcast_fusion.13), channel_id=1, source_target_pairs={{0,4},{1,5},{2,6},{3,7},{4,0},{5,1},{6,2},{7,3},{8,12},{9,13},{10,... | collective-permute-start | bytes 1105928 | tf_op jit(solution)/shard_map/ppermute | solution.py:303
  460.1 12.1 %collective-permute-start.12 = (bf16[4,24,2048]{2,1,0:T(8,128)(2,1)}, bf16[4,24,2048]{2,1,0:T(8,128)(2,1)}, u32[]{:S(2)}, u32[]{:S(2)}) collective-permute-start(bf16[4,24,2048]{2,1,0:T(8,128)(2,1)} %dynamic-slice_bitcast_fusion.12), channel_id=1, source_target_pairs={{0,2},{1,3},{2,0},{3,1},{4,6},{5,7},{6,4},{7,5},{8,10},{9,11},{10,... | collective-permute-start | bytes 1179656 | tf_op jit(solution)/shard_map/ppermute | solution.py:303
  467.1 16.1 %all-to-all-start.8 = ((bf16[4,24,1920]{2,1,0:T(8,128)(2,1)}), bf16[4,24,1920]{2,1,0:T(8,128)(2,1)S(1)}, u32[]{:S(2)}, u32[]{:S(2)}) async-start(bf16[4,24,1920]{2,1,0:T(8,128)(2,1)} %fusion.45), calls=%async_computation.8 | async-start | bytes 737280 | tf_op jit(solution)/shard_map/all_to_all | solution.py:330
  483.2 32.4 %all-to-all-start.7 = ((bf16[4,24,2048]{2,1,0:T(8,128)(2,1)}), bf16[4,24,2048]{2,1,0:T(8,128)(2,1)S(1)}, u32[]{:S(2)}, u32[]{:S(2)}) async-start(bf16[4,24,2048]{2,1,0:T(8,128)(2,1)} %fusion.41), calls=%async_computation.7 | async-start | bytes 786432 | tf_op jit(solution)/shard_map/all_to_all | solution.py:330
  (81 other events, 635.7 us)

commit v2 on v1

v2 whole, which is shorter than its diff:
```python
import functools

import jax
import jax.numpy as jnp
from jax import lax
from jax.experimental import pallas as pl
from jax.experimental.pallas import tpu as pltpu
from jax.sharding import PartitionSpec as P

HEAD_DIM = 32
TEXT_VOCAB = 32000
BLOCK = 256
HEADS_STEP = 2
MESH = pl.DeviceIdType.MESH
LOG2_E = 1.4426950408889634


def normalize(values):
    average = jnp.mean(values, -1, keepdims=True)
    centred = values - average
    variance = jnp.mean(centred * centred, -1, keepdims=True)
    return centred * lax.rsqrt(variance + 1e-05)


def norm_affine(values, gain, offset):
    return normalize(values) * gain + offset


def contract(left, right, left_dim, right_dim):
    return lax.dot_general(
        left, right, (((left_dim,), (right_dim,)), ((), ())), preferred_element_type=jnp.float32
    )


def product(left, right):
    return contract(left, right, 1, 0)


def product_left(left, right):
    return contract(left, right, 0, 0)


def product_right(left, right):
    return contract(left, right, 1, 1)


def forward_kernel(heads, q_ref, k_ref, v_ref, o_ref, p_ref, r_ref):
    length = q_ref.shape[1]
    scaling = HEAD_DIM ** (-0.5) * LOG2_E
    key_place = lax.broadcasted_iota(jnp.int32, (BLOCK, BLOCK), 0)
    query_place = lax.broadcasted_iota(jnp.int32, (BLOCK, BLOCK), 1)
    allowed = key_place <= query_place
    for head in range(heads):
        rows = slice(head * HEAD_DIM, (head + 1) * HEAD_DIM)
        keys = k_ref[rows, :]
        values = v_ref[rows, :]
        for step in range(length // BLOCK):
            start, end = step * BLOCK, (step + 1) * BLOCK
            scores = contract(keys[:, :end], q_ref[rows, start:end], 0, 0) * scaling
            corner = jnp.where(allowed, scores[start:], -1e30)
            highest = jnp.max(corner, 0, keepdims=True)
            if step:
                highest = jnp.maximum(highest, jnp.max(scores[:start], 0, keepdims=True))
            weights = jnp.exp2(corner - highest)
            total = jnp.sum(weights, 0, keepdims=True)
            weights = weights.astype(jnp.bfloat16)
            if step:
                above = jnp.exp2(scores[:start] - highest)
                total = total + jnp.sum(above, 0, keepdims=True)
                weights = jnp.concatenate([above.astype(jnp.bfloat16), weights], 0)
            inverse = 1.0 / total
            base = BLOCK * (step * (step + 1) // 2)
            p_ref[head, base : base + end, :] = weights
            r_ref[head, :, start:end] = inverse
            o_ref[rows, start:end] = (
                contract(values[:, :end], weights, 1, 0) * inverse
            ).astype(jnp.bfloat16)


def packed_rows(length):
    steps = length // BLOCK
    return BLOCK * (steps * (steps + 1) // 2)


def attention_forward(queries, key_heads, values):
    width, length = queries.shape
    heads = width // HEAD_DIM
    packed = packed_rows(length)
    rows = pl.BlockSpec((HEADS_STEP * HEAD_DIM, length), lambda g: (g, 0))
    return pl.pallas_call(
        functools.partial(forward_kernel, HEADS_STEP),
        grid=(heads // HEADS_STEP,),
        in_specs=[rows] * 3,
        out_specs=[
            rows,
            pl.BlockSpec((HEADS_STEP, packed, BLOCK), lambda g: (g, 0, 0)),
            pl.BlockSpec((HEADS_STEP, 1, length), lambda g: (g, 0, 0)),
        ],
        out_shape=[
            jax.ShapeDtypeStruct((width, length), jnp.bfloat16),
            jax.ShapeDtypeStruct((heads, packed, BLOCK), jnp.bfloat16),
            jax.ShapeDtypeStruct((heads, 1, length), jnp.float32),
        ],
        compiler_params=pltpu.CompilerParams(vmem_limit_bytes=32 << 20),
        cost_estimate=pl.CostEstimate(
            flops=50_000_000_000, bytes_accessed=heads * packed * BLOCK * 2, transcendentals=0
        ),
        name="attention_forward",
    )(queries, key_heads, values)


def backward_kernel(heads, count, q_ref, k_ref, v_ref, o_ref, g_ref, p_ref, r_ref, *refs):
    packs, d_ref, outs = refs[:count], refs[count], refs[count + 1 : 2 * count + 1]
    s_ref = refs[2 * count + 1]
    shares = shares_of(packs, outs, refs[2 * count + 2 :])
    bits = shares[0].bits
    first, second = shares
    number = pl.program_id(0)
    last = pl.num_programs(0) - 1

    @pl.when(number == 0)
    def begin():
        greet(False)
        first.start()
        second.start()

    @pl.when(number == 2)
    def begin_first():
        first.take(0)

    @pl.when(number == 5)
    def begin_second():
        first.take(1)
        second.take(0)

    @pl.when(number == 8)
    def go_on():
        for stage in range(2, bits):
            first.take(stage)

    length = q_ref.shape[1]
    steps = length // BLOCK
    scaling = HEAD_DIM ** (-0.5)
    for head in range(heads):
        rows = slice(head * HEAD_DIM, (head + 1) * HEAD_DIM)
        grads = (g_ref[rows, :].astype(jnp.float32) * r_ref[head]).astype(jnp.bfloat16)
        inner = jnp.sum(
            grads.astype(jnp.float32) * o_ref[rows, :].astype(jnp.float32), 0, keepdims=True
        )
        queries = q_ref[rows, :]
        keys = k_ref[rows, :]
        values = v_ref[rows, :]
        for step in range(steps):
            start, end = step * BLOCK, (step + 1) * BLOCK
            base = BLOCK * (step * (step + 1) // 2)
            grad_probs = contract(values[:, :end], grads[:, start:end], 0, 0)
            grad_scores = p_ref[head, base : base + end, :] * (
                grad_probs - inner[:, start:end]
            ).astype(jnp.bfloat16)
            s_ref[head, base : base + end, :] = grad_scores
            d_ref[0, rows, start:end] = (
                contract(keys[:, :end], grad_scores, 1, 0) * scaling
            ).astype(jnp.bfloat16)
        for column in range(steps):
            grad_keys = jnp.zeros((HEAD_DIM, BLOCK), jnp.float32)
            grad_values = jnp.zeros((HEAD_DIM, BLOCK), jnp.float32)
            for step in range(column, steps):
                base = BLOCK * (step * (step + 1) // 2 + column)
                span = slice(step * BLOCK, (step + 1) * BLOCK)
                grad_values = grad_values + contract(
                    grads[:, span], p_ref[head, base : base + BLOCK, :], 1, 1
                )
                grad_keys = grad_keys + contract(
                    queries[:, span], s_ref[head, base : base + BLOCK, :], 1, 1
                )
            span = slice(column * BLOCK, (column + 1) * BLOCK)
            d_ref[1, rows, span] = (grad_keys * scaling).astype(jnp.bfloat16)
            d_ref[2, rows, span] = grad_values.astype(jnp.bfloat16)

    @pl.when(number == last)
    def end():
        for stage in range(1, bits):
            second.take(stage)
        first.finish()
        second.finish()


def attention_backward(queries, key_heads, values, attended, grads, probs, inverse, packs):
    width, length = queries.shape
    heads = width // HEAD_DIM
    packed = packed_rows(length)
    rows = pl.BlockSpec((HEADS_STEP * HEAD_DIM, length), lambda g: (g, 0))
    scratch = [pltpu.VMEM((HEADS_STEP, packed, BLOCK), jnp.bfloat16)]
    for pack in packs:
        scratch = scratch + shares_scratch(pack.shape)
    return pl.pallas_call(
        functools.partial(backward_kernel, HEADS_STEP, len(packs)),
        grid=(heads // HEADS_STEP,),
        in_specs=[rows] * 5
        + [
            pl.BlockSpec((HEADS_STEP, packed, BLOCK), lambda g: (g, 0, 0)),
            pl.BlockSpec((HEADS_STEP, 1, length), lambda g: (g, 0, 0)),
        ]
        + [pl.BlockSpec(memory_space=pl.ANY)] * len(packs),
        out_specs=[pl.BlockSpec((3, HEADS_STEP * HEAD_DIM, length), lambda g: (0, g, 0))]
        + [pl.BlockSpec(pack.shape[-2:], lambda g: (0, 0)) for pack in packs],
        out_shape=[jax.ShapeDtypeStruct((3, width, length), jnp.bfloat16)]
        + [jax.ShapeDtypeStruct(pack.shape[-2:], jnp.float32) for pack in packs],
        scratch_shapes=scratch,
        compiler_params=pltpu.CompilerParams(
            collective_id=2, has_side_effects=True, vmem_limit_bytes=56 << 20
        ),
        name="attention_backward",
    )(queries, key_heads, values, attended, grads, probs, inverse, *packs)


def bit_of(index, bit):
    return lax.rem(lax.div(index, 1 << bit), 2)


def flipped(index, bit):
    return index + (1 - 2 * bit_of(index, bit)) * (1 << bit)


def spans_of(rows):
    first = (rows + 31) // 32 * 16
    return ((0, first), (first, rows - first))


class Shares:
    def __init__(self, pack, out, refs):
        self.pack, self.out = pack, out
        self.groups = pack.shape[0]
        self.bits = len(pack.shape) - 3
        self.spans = spans_of(pack.shape[-2])
        refs = list(refs)
        self.own, self.zero = refs[:2]
        count = self.bits - 1
        self.later = [refs[2 + half * count : 2 + (half + 1) * count] for half in range(2)]
        refs = refs[2 + 2 * count :]
        self.ring = refs[:2]
        self.local_sem, self.swap_send, self.swap_got, self.ring_send, self.ring_got = refs[2:]
        self.emb = lax.axis_index("emb")
        self.group = lax.axis_index("dp")
        self.every = (slice(None),) * self.bits

    def order(self, half):
        rest = list(range(1, self.bits))
        return [0] + (rest if half == 0 else rest[::-1])

    def span(self, half):
        return pl.ds(*self.spans[half])

    def place(self, half, stage, mine):
        order = self.order(half)
        index = []
        for bit in range(self.bits - 1, 0, -1):
            value = bit_of(self.emb, bit)
            if order.index(bit) < stage:
                index.append(value)
            elif order.index(bit) == stage:
                index.append(value if mine else 1 - value)
            else:
                index.append(slice(None))
        return tuple(index)

    def swap(self, half, stage):
        if stage == 0:
            other = 1 - bit_of(self.emb, 0)
            source = self.pack.at[self.every + (other, self.span(half))]
            target = self.zero.at[self.every + (self.span(half),)]
        else:
            place = self.place(half, stage, False)
            source = self.own.at[(slice(None),) + place + (self.span(half),)]
            target = self.later[half][stage - 1]
        return pltpu.make_async_remote_copy(
            src_ref=source,
            dst_ref=target,
            send_sem=self.swap_send.at[half, stage],
            recv_sem=self.swap_got.at[half, stage],
            device_id={"emb": flipped(self.emb, self.order(half)[stage])},
            device_id_type=MESH,
        )

    def bring(self, half):
        mine = bit_of(self.emb, 0)
        return pltpu.make_async_copy(
            self.pack.at[self.every + (mine, self.span(half))],
            self.own.at[self.every + (self.span(half),)],
            self.local_sem.at[half],
        )

    def hop(self, half, step):
        other = lax.rem(self.group + step, self.groups)
        place = (other,) + self.place(half, self.bits, True) + (self.span(half),)
        return pltpu.make_async_remote_copy(
            src_ref=self.own.at[place],
            dst_ref=self.ring[half].at[step - 1],
            send_sem=self.ring_send.at[half, step - 1],
            recv_sem=self.ring_got.at[half, step - 1],
            device_id={"dp": other},
            device_id_type=MESH,
        )

    def start(self):
        for half in range(2):
            self.swap(half, 0).start()
            self.bring(half).start()

    def take(self, stage):
        for half in range(2):
            self.take_half(half, stage)

    def take_half(self, half, stage):
        if stage == 0:
            self.bring(half).wait()
        self.swap(half, stage).wait()
        place = self.place(half, stage, True)
        free = [n for n, index in enumerate(place) if isinstance(index, slice)]

        def one(number, carry):
            group = lax.rem(number, self.groups)
            rest = lax.div(number, self.groups)
            index = list(place)
            there = []
            for n in free:
                index[n] = lax.rem(rest, 2)
                there.append(index[n])
                rest = lax.div(rest, 2)
            target = (group,) + tuple(index) + (self.span(half), slice(None))
            if stage == 0:
                arrived = self.zero[target]
            else:
                arrived = self.later[half][stage - 1][(group,) + tuple(there)]
            total = self.own[target].astype(jnp.float32) + arrived.astype(jnp.float32)
            self.own[target] = total.astype(jnp.bfloat16)
            return carry

        lax.fori_loop(0, self.groups * 2 ** len(free), one, 0)
        if stage + 1 < self.bits:
            self.swap(half, stage + 1).start()
        else:
            for step in range(1, self.groups):
                self.hop(half, step).start()

    def finish(self):
        for half in range(2):
            place = (self.group,) + self.place(half, self.bits, True)
            total = self.own[place + (self.span(half), slice(None))].astype(jnp.float32)
            for step in range(1, self.groups):
                self.hop(half, step).wait()
                total = total + self.ring[half][step - 1].astype(jnp.float32)
            self.out[self.span(half), :] = total


def shares_scratch(shape):
    groups, bits, columns = shape[0], len(shape) - 3, shape[-1]
    whole = pltpu.VMEM((groups,) + (2,) * (bits - 1) + shape[-2:], jnp.bfloat16)
    later = [
        pltpu.VMEM((groups,) + (2,) * (bits - 1 - stage) + (span[1], columns), jnp.bfloat16)
        for span in spans_of(shape[-2])
        for stage in range(1, bits)
    ]
    ring = [
        pltpu.VMEM((groups - 1, span[1], columns), jnp.bfloat16) for span in spans_of(shape[-2])
    ]
    semaphores = [(2,), (2, bits), (2, bits), (2, groups - 1), (2, groups - 1)]
    return [whole, whole, *later, *ring] + [pltpu.SemaphoreType.DMA(size) for size in semaphores]


def shares_of(packs, outs, refs):
    bits = len(packs[0].shape) - 3
    each = 2 + 2 * (bits - 1) + 2 + 5
    return [
        Shares(pack, out, refs[n * each : (n + 1) * each])
        for n, (pack, out) in enumerate(zip(packs, outs))
    ]


def greet(everyone):
    emb, group = lax.axis_index("emb"), lax.axis_index("dp")
    owners, groups = lax.axis_size("emb"), lax.axis_size("dp")
    barrier = pltpu.get_barrier_semaphore()
    if everyone:
        others = [lax.rem(emb + step, owners) for step in range(1, owners)]
    else:
        others = [flipped(emb, bit) for bit in range(owners.bit_length() - 1)]
    for other in others:
        pl.semaphore_signal(barrier, inc=1, device_id={"emb": other}, device_id_type=MESH)
    for step in range(1, groups):
        other = lax.rem(group + step, groups)
        pl.semaphore_signal(barrier, inc=1, device_id={"dp": other}, device_id_type=MESH)
    pl.semaphore_wait(barrier, len(others) + groups - 1)


def blocks_of(array):
    owners, groups = lax.axis_size("emb"), lax.axis_size("dp")
    bits = owners.bit_length() - 1
    return array.reshape((groups,) + (2,) * bits + array.shape[1:])


def rows_of(array):
    devices = lax.axis_size("emb") * lax.axis_size("dp")
    return array.astype(jnp.bfloat16).reshape(devices, array.shape[0] // devices, array.shape[1])


def stacked(pieces):
    rows = sum(piece.shape[1] for piece in pieces)
    devices, _, columns = pieces[0].shape
    spare = -rows % 16
    if rows + spare < 32:
        spare = 32 - rows
    if spare:
        pieces = pieces + [jnp.zeros((devices, spare, columns), jnp.bfloat16)]
    return blocks_of(jnp.concatenate(pieces, 1))


def vector_rows(vectors, rows):
    devices = lax.axis_size("emb") * lax.axis_size("dp")
    wide = vectors[0].shape[0]
    piece = jnp.stack(vectors).astype(jnp.bfloat16).reshape(len(vectors), devices, -1)
    piece = jnp.swapaxes(piece, 0, 1).reshape(devices, 1, -1)
    return jnp.pad(piece, ((0, 0), (0, rows - 1), (0, wide - piece.shape[2])))


def table_scratch(groups, owners, columns, length, capacity):
    wide = groups * capacity
    return [
        pltpu.VMEM((groups, columns, length), jnp.bfloat16),
        pltpu.VMEM((owners, columns, wide), jnp.bfloat16),
        pltpu.VMEM((owners - 1, columns, wide), jnp.bfloat16),
        pltpu.SemaphoreType.DMA((1,)),
        pltpu.SemaphoreType.DMA((groups - 1,)),
        pltpu.SemaphoreType.DMA((groups - 1,)),
        pltpu.SemaphoreType.DMA((owners - 1,)),
        pltpu.SemaphoreType.DMA((owners - 1,)),
    ]


class Table:
    def __init__(self, grads, slots, ids, out, refs):
        self.grads, self.slots, self.ids, self.out = grads, slots, ids, out
        self.turned, self.packed, self.landed = refs[:3]
        self.local_sem, self.ring_send, self.ring_got, self.send, self.got = refs[3:]
        self.groups, self.columns, self.length = self.turned.shape
        self.owners, _, self.wide = self.packed.shape
        self.capacity = self.wide // self.groups
        self.emb = lax.axis_index("emb")
        self.group = lax.axis_index("dp")

    def bring(self):
        return pltpu.make_async_copy(
            self.grads.at[self.group], self.turned.at[0], self.local_sem.at[0]
        )

    def hop(self, step):
        other = lax.rem(self.group + step, self.groups)
        return pltpu.make_async_remote_copy(
            src_ref=self.grads.at[other],
            dst_ref=self.turned.at[step],
            send_sem=self.ring_send.at[step - 1],
            recv_sem=self.ring_got.at[step - 1],
            device_id={"dp": other},
            device_id_type=MESH,
        )

    def give(self, step):
        other = lax.rem(self.emb + step, self.owners)
        return pltpu.make_async_remote_copy(
            src_ref=self.packed.at[other],
            dst_ref=self.landed.at[step - 1],
            send_sem=self.send.at[step - 1],
            recv_sem=self.got.at[step - 1],
            device_id={"emb": other},
            device_id_type=MESH,
        )

    def start(self):
        self.bring().start()
        for step in range(1, self.groups):
            self.hop(step).start()

    def arrive(self):
        self.bring().wait()
        for step in range(1, self.groups):
            self.hop(step).wait()

    def sort(self, step):
        owner = lax.rem(self.emb + step, self.owners)
        lanes = lax.broadcasted_iota(jnp.int32, (self.length, 128), 1)
        tiles = []
        for tile in range(self.wide // 128):
            total = jnp.zeros((self.columns, 128), jnp.float32)
            for group in range(self.groups):
                low, high = group * self.capacity, (group + 1) * self.capacity
                if high <= tile * 128 or low >= (tile + 1) * 128:
                    continue
                source = lax.rem(self.group - group + self.groups, self.groups)
                slot = lanes + (tile * 128 - low)
                inside = (slot >= 0) & (slot < self.capacity)
                wanted = jnp.where(inside, slot + owner * self.capacity, -2)
                hot = jnp.where(wanted == self.slots[source], 1.0, 0.0).astype(jnp.bfloat16)
                total = total + product(self.turned[group], hot)
            tiles.append(total.astype(jnp.bfloat16))
        self.packed[owner] = jnp.concatenate(tiles, 1)
        return owner

    def add(self, step, first):
        source = lax.rem(self.emb - step + self.owners, self.owners)
        rows, columns = self.out.shape
        count = 6 if rows % 48 == 0 else 1
        block = rows // count
        chunk = self.packed[self.emb] if step == 0 else self.landed[step - 1]

        def one(number, carry):
            base = pl.multiple_of(number * block, 8)
            places = base + lax.broadcasted_iota(jnp.int32, (block, self.wide), 0)
            hot = jnp.where(places == self.ids[source], 1.0, 0.0).astype(jnp.bfloat16)
            part = product_right(hot, chunk)
            if not first:
                part = part + self.out[pl.ds(base, block), :]
            self.out[pl.ds(base, block), :] = part
            return carry

        lax.fori_loop(0, count, one, 0)


def tail_kernel(count, grads_ref, slots_ref, ids_ref, *refs):
    packs, table_out, outs = refs[:count], refs[count], refs[count + 1 : 2 * count + 1]
    refs = refs[2 * count + 1 :]
    table = Table(grads_ref, slots_ref, ids_ref, table_out, refs[:8])
    shares = shares_of(packs, outs, refs[8:])
    owners = table.owners
    greet(True)
    table.start()
    for share in shares:
        share.start()
    shares[0].take(0)
    shares[1].take(0)
    for stage in range(1, shares[0].bits):
        for share in shares:
            share.take(stage)
    table.arrive()
    for step in range(1, owners):
        table.sort(step)
        table.give(step).start()
    table.sort(0)
    table.add(0, True)
    for share in shares:
        share.finish()
    for step in range(1, owners):
        table.give(step).wait()
        table.add(step, False)


def tail(grads, slots, ids, packs, table_rows, capacity):
    groups, columns, length = grads.shape
    owners = ids.shape[0]
    anywhere = pl.BlockSpec(memory_space=pl.ANY)
    vmem = pl.BlockSpec(memory_space=pltpu.VMEM)
    scratch = table_scratch(groups, owners, columns, length, capacity)
    for pack in packs:
        scratch = scratch + shares_scratch(pack.shape)
    return pl.pallas_call(
        functools.partial(tail_kernel, len(packs)),
        in_specs=[anywhere, vmem, vmem] + [anywhere] * len(packs),
        out_specs=[vmem] * (1 + len(packs)),
        out_shape=[jax.ShapeDtypeStruct((table_rows, columns), jnp.float32)]
        + [jax.ShapeDtypeStruct(pack.shape[-2:], jnp.float32) for pack in packs],
        scratch_shapes=scratch,
        compiler_params=pltpu.CompilerParams(
            collective_id=3, has_side_effects=True, vmem_limit_bytes=56 << 20
        ),
        name="tail",
    )(grads, slots, ids, *packs)


def on_device(
    pixels,
    counts,
    token_ids,
    action_bins,
    patch_pos,
    token_table,
    pos_table,
    w_patch,
    w_res_a,
    w_res_b,
    gain_one,
    bias_one,
    w_q,
    w_k,
    w_v,
    w_o,
    gain_two,
    bias_two,
    w_up,
    w_down,
    cotangent,
):
    length = pixels.shape[0]
    model_width = w_q.shape[0]
    positions = jnp.arange(length)
    image_rows = positions < counts[0, 0]
    action_rows = positions >= length - counts[0, 1]
    table_rows = jnp.logical_not(image_rows)
    row_ids = jnp.where(action_rows, TEXT_VOCAB + action_bins, token_ids)
    rows_owned = token_table.shape[0]
    owners_total = lax.axis_size("emb")
    capacity = 3 * length // (2 * owners_total)
    owner_index = row_ids // rows_owned
    local_row = row_ids - owner_index * rows_owned
    owner_hot = (
        (owner_index[:, None] == jnp.arange(owners_total)[None, :]) & table_rows[:, None]
    ).astype(jnp.int32)
    earlier = jnp.cumsum(owner_hot, 0) - owner_hot
    rank_within = jnp.sum(earlier * owner_hot, 1)
    slot_index = jnp.where(
        table_rows, owner_index * capacity + rank_within, owners_total * capacity
    )
    request = (
        jnp.full((owners_total * capacity + 1,), -1, jnp.int32)
        .at[slot_index]
        .set(jnp.where(table_rows, local_row, -1))
    )
    received = lax.all_to_all(
        request[:-1].reshape(owners_total, capacity), "emb", split_axis=0, concat_axis=0, tiled=True
    )
    valid_slots = received >= 0
    local_ids = jnp.maximum(received, 0)
    fetched = jnp.where(valid_slots[..., None], token_table[local_ids], jnp.zeros((), jnp.bfloat16))
    returned = lax.all_to_all(fetched, "emb", split_axis=0, concat_axis=0, tiled=True)
    slot_safe = jnp.minimum(slot_index, owners_total * capacity - 1)
    table_embed = returned.reshape(owners_total * capacity, model_width)[slot_safe].astype(
        jnp.float32
    )
    patch_first = product(pixels, w_patch)
    first_low = patch_first.astype(jnp.bfloat16)
    res_inner = product(first_low, w_res_a)
    res_gelu, gelu_back_res = jax.vjp(jax.nn.gelu, res_inner)
    res_act = res_gelu.astype(jnp.bfloat16)
    res_mixed = product(res_act, w_res_b)
    position_hot = patch_pos[:, None] == jnp.arange(pos_table.shape[0])[None, :]
    position_embed = product(position_hot.astype(jnp.bfloat16), pos_table)
    image_embed = patch_first + res_mixed + position_embed
    embedded = jnp.where(image_rows[:, None], image_embed, table_embed)
    normed_one_f, norm_back_one = jax.vjp(
        norm_affine, embedded, gain_one.astype(jnp.float32), bias_one.astype(jnp.float32)
    )
    normed_one = normed_one_f.astype(jnp.bfloat16)
    queries = contract(w_q, normed_one, 0, 1).astype(jnp.bfloat16)
    key_heads = contract(w_k, normed_one, 0, 1).astype(jnp.bfloat16)
    value_heads = contract(w_v, normed_one, 0, 1).astype(jnp.bfloat16)
    attended, probs, inverse = attention_forward(queries, key_heads, value_heads)
    middle = embedded + product_left(attended, w_o)
    normed_two_f, norm_back_two = jax.vjp(
        norm_affine, middle, gain_two.astype(jnp.float32), bias_two.astype(jnp.float32)
    )
    normed_two = normed_two_f.astype(jnp.bfloat16)
    up_pre = product(normed_two, w_up)
    up_act, gelu_back_up = jax.vjp(jax.nn.gelu, up_pre)
    up_low = up_act.astype(jnp.bfloat16)
    output = (middle + product(up_low, w_down)).astype(jnp.bfloat16)
    grad_w_down = product_left(up_low, cotangent)
    (grad_up_pre,) = gelu_back_up(product_right(cotangent, w_down))
    grad_up = grad_up_pre.astype(jnp.bfloat16)
    grad_w_up = product_left(normed_two, grad_up).astype(jnp.bfloat16)
    devices = lax.axis_size("dp") * owners_total
    share = model_width // devices
    folds = grad_w_up.shape[1] // model_width
    folded = grad_w_up.reshape(devices, share, folds, model_width)
    folded = jnp.swapaxes(folded, 1, 2).reshape(devices, folds * share, model_width)
    grad_normed_two = product_right(grad_up, w_up)
    grad_middle_norm, grad_gain_two, grad_bias_two = norm_back_two(grad_normed_two)
    grad_middle = cotangent.astype(jnp.float32) + grad_middle_norm
    grad_branch = grad_middle.astype(jnp.bfloat16)
    grad_w_o = product(attended, grad_branch)
    grad_attended = product_right(w_o, grad_branch).astype(jnp.bfloat16)
    gains_two = vector_rows([grad_gain_two, grad_bias_two], 8)
    grad_heads, share_down, share_up = attention_backward(
        queries,
        key_heads,
        value_heads,
        attended,
        grad_attended,
        probs,
        inverse,
        [stacked([rows_of(grad_w_down)]), stacked([folded, rows_of(grad_w_o), gains_two])],
    )
    grad_heads = grad_heads.reshape(3 * model_width, length)
    grad_normed_one = product_left(grad_heads, jnp.concatenate([w_q.T, w_k.T, w_v.T], 0))
    grad_embed_norm, grad_gain_one, grad_bias_one = norm_back_one(grad_normed_one)
    gains_one = vector_rows([grad_gain_one, grad_bias_one], 8)
    grad_w_heads = [
        rows_of(contract(normed_one, grad_heads[n * model_width : (n + 1) * model_width], 0, 1))
        for n in range(3)
    ]
    grad_embedded = grad_middle + grad_embed_norm
    grad_low = grad_embedded.astype(jnp.bfloat16)
    groups = lax.axis_size("dp")
    columns = model_width // groups
    all_ids = lax.all_gather(received, "dp", axis=0, tiled=False)
    all_ids = jnp.swapaxes(all_ids, 0, 1)
    turned = (groups - jnp.arange(groups) + lax.axis_index("dp")) % groups
    all_ids = all_ids[:, turned].reshape(owners_total, 1, groups * capacity)
    all_slots = lax.all_gather(slot_index, "dp", axis=0, tiled=False)[:, :, None]
    grads_turned = grad_low.T.reshape(groups, columns, length)
    grad_image = jnp.where(image_rows[:, None], grad_embedded, 0.0)
    grad_mixed = grad_image.astype(jnp.bfloat16)
    grad_pos_table = product_left(position_hot.astype(jnp.bfloat16), grad_mixed)
    grad_w_res_b = product_left(res_act, grad_mixed)
    (grad_inner_f,) = gelu_back_res(product_right(grad_mixed, w_res_b))
    grad_inner = grad_inner_f.astype(jnp.bfloat16)
    grad_w_res_a = product_left(first_low, grad_inner)
    grad_first = (grad_image + product_right(grad_inner, w_res_a)).astype(jnp.bfloat16)
    grad_w_patch = product_left(pixels, grad_first)
    grad_pixels = product_right(grad_first, w_patch)
    res_rows = [rows_of(g) for g in (grad_w_patch, grad_w_res_a, grad_w_res_b, grad_pos_table)]
    grad_table, share_heads, share_res = tail(
        grads_turned,
        all_slots,
        all_ids,
        [stacked(grad_w_heads + [gains_one]), stacked(res_rows)],
        rows_owned,
        capacity,
    )
    pos_share = pos_table.shape[0] // devices
    wide = folds * share

    def cut(array, place):
        return array[place * share : (place + 1) * share]

    share_w_up = jnp.swapaxes(share_up[:wide].reshape(folds, share, model_width), 0, 1)
    gains_two = share_up[wide + share, : 2 * share]
    gains_one = share_heads[3 * share, : 2 * share]
    return (
        output,
        grad_pixels,
        grad_table,
        share_res[3 * share : 3 * share + pos_share],
        cut(share_res, 0),
        cut(share_res, 1),
        cut(share_res, 2),
        gains_one[:share],
        gains_one[share:],
        cut(share_heads, 0),
        cut(share_heads, 1),
        cut(share_heads, 2),
        share_up[wide : wide + share],
        gains_two[:share],
        gains_two[share:],
        share_w_up.reshape(share, folds * model_width),
        share_down[: grad_w_down.shape[0] // devices],
    )


def solution(mesh):
    in_specs = (
        P(("dp", "emb"), None),
        P(("dp", "emb"), None),
        P(("dp", "emb")),
        P(("dp", "emb")),
        P(("dp", "emb")),
        P("emb", None),
        P(),
        P(),
        P(),
        P(),
        P(),
        P(),
        P(),
        P(),
        P(),
        P(),
        P(),
        P(),
        P(),
        P(),
        P(("dp", "emb"), None),
    )
    out_specs = (
        P(("dp", "emb"), None),
        P(("dp", "emb"), None),
        P("emb", "dp"),
        P(("dp", "emb"), None),
        P(("dp", "emb"), None),
        P(("dp", "emb"), None),
        P(("dp", "emb"), None),
        P(("dp", "emb")),
        P(("dp", "emb")),
        P(("dp", "emb"), None),
        P(("dp", "emb"), None),
        P(("dp", "emb"), None),
        P(("dp", "emb"), None),
        P(("dp", "emb")),
        P(("dp", "emb")),
        P(("dp", "emb"), None),
        P(("dp", "emb"), None),
    )
    return jax.shard_map(
        on_device, mesh=mesh, in_specs=in_specs, out_specs=out_specs, check_vma=False
    )
```

time: 527 us -> 482 us (0.915)
  the two profiles are of different devices: /device:TPU:0 before, /device:TPU:9 now
where the time goes in v2:
time: 482 us; the launch traced here: 473 us
  Pallas kernels  220 us (46%)
  matrix products  116 us (24%)
  local copies, waits for them, and re-layouts  71.2 us (15%)
  blocking collectives  29 us (6%)
  other arithmetic  28.8 us (6%)
  starting transfers between devices  5.11 us (1%)
    dot_general x27, matrix products, contract(): lax.dot_general(left, right, (((left_dim,), (right_dim,)), ((), ())), pre...  116 us
    pallas_call x1, Pallas kernels, tail(): pl.pallas_call(functools.partial(tail_kernel, len(packs)), in_specs=[anyw...  91.9 us
    pallas_call x1, Pallas kernels, attention_backward(): pl.pallas_call(functools.partial(backward_kernel, HEADS_STEP, len(packs))...  83.1 us
    pallas_call x1, Pallas kernels, attention_forward(): pl.pallas_call(functools.partial(forward_kernel, HEADS_STEP), grid=(heads...  45.4 us
    unnamed x123, local copies, waits for them, and re-layouts  17.3 us
    reshape x2, local copies, waits for them, and re-layouts, on_device(): folded = grad_w_up.reshape(devices, share, folds, model_width)  15.1 us
    all_gather x1, blocking collectives, on_device(): lax.all_gather(slot_index, 'dp', axis=0, tiled=False)[:, :, None]  10.8 us
    concatenate x3, other arithmetic, stacked(): return blocks_of(jnp.concatenate(pieces, 1))  10.7 us
  transfers between devices with their start and end apart: 1, of which 0 were waited for; matrix products, arithmetic and copies ran while one was open for 3% of the time, Pallas kernels for 0%

profile of v2, /device:TPU:9, one launch (start us, length us, event | category | flops | bytes accessed | tf_op | source)
XLA Modules:
  0.0 473.3 jit_solution(18181914994785392251)
XLA Ops:
  8.9 4.3 scatter_custom_fusion
  13.3 8.2 %all_to_all.14 = s32[8,1,192]{2,1,0:T(1,128)S(1)} all-to-all(s32[8,1,192]{2,1,0:T(1,128)S(1)} %all_to_all.9), channel_id=1, replica_groups=mesh['dp'=4,'emb'=8] {'emb'}, dimensions={0} | all-to-all | bytes 12288 | tf_op jit(solution)/shard_map/all_to_all | solution.py:626
  21.6 10.3 %gather_fusion = bf16[1536,768]{1,0:T(8,128)(2,1)} fusion(bf16[4128,768]{1,0:T(8,128)(2,1)} %param.26, s32[2048]{0:T(1024)S(1)} %pad_clamp_fusion), kind=kCustom, calls=%fused_computation | custom fusion | bytes 4724736 | tf_op jit(solution)/shard_map/gather | solution.py:631
  31.9 3.4 broadcast_select_fusion
  35.3 5.1 %all-to-all-start.1 = ((bf16[8,192,768]{2,1,0:T(8,128)(2,1)}), bf16[8,192,768]{2,1,0:T(8,128)(2,1)}, u32[]{:S(2)}, u32[]{:S(2)}) async-start(bf16[8,192,768]{2,1,0:T(8,128)(2,1)} %broadcast_select_fusion), calls=%async_computation.1 | async-start | bytes 4718592 | tf_op jit(solution)/shard_map/all_to_all | solution.py:632
  42.1 10.8 %all-gather = s32[4096]{0:T(1024)S(1)} all-gather(s32[1024]{0:T(1024)S(1)} %get-tuple-element.131), channel_id=2, replica_groups=mesh['dp'=4,'emb'=8] {'dp'}, dimensions={0}, use_global_device_ids=true | all-gather | bytes 20480 | tf_op jit(solution)/shard_map/all_gather | solution.py:706
  52.9 3.3 broadcast_in_dim.90.slots_ref
  57.5 2.8 fusion.77
  63.4 3.3 fusion.68
  66.7 10.1 %all-gather.1 = s32[32,1,192]{2,1,0:T(1,128)S(1)} all-gather(s32[8,1,192]{2,1,0:T(1,128)S(1)} %all_to_all.14), channel_id=3, replica_groups=mesh['dp'=4,'emb'=8] {'dp'}, dimensions={0}, use_global_device_ids=true | all-gather | bytes 30720 | tf_op jit(solution)/shard_map/all_gather | solution.py:702
  78.1 7.5 %gather_fusion.1 = bf16[1024,768]{1,0:T(8,128)(2,1)} fusion(bf16[1536,768]{1,0:T(8,128)(2,1)} %bitcast.6, s32[1024]{0:T(1024)S(1)} %get-tuple-element.130), kind=kCustom, calls=%fused_computation.1 | custom fusion | bytes 3149824 | tf_op jit(solution)/shard_map/gather | solution.py:634
  87.4 3.8 fusion.75
  98.8 45.4 %attention_forward.1 = (bf16[768,1024]{1,0:T(8,128)(2,1)S(1)}, bf16[24,2560,256]{2,1,0:T(8,128)(2,1)}, f32[24,1,1024]{2,1,0:T(1,128)S(1)}) custom-call(bf16[768,1024]{1,0:T(8,128)(2,1)S(1)} %fusion.39.q_ref, bf16[768,1024]{1,0:T(8,128)(2,1)S(1)} %fusion.40.k_ref, bf16[768,1024]{1,0:T(8,128)(2,1)S(1)} %fusion.41.v_ref), custom_call_target="tpu_custom_call" | custom-call | flops 49999998976 | bytes 31457280 | tf_op jit(solution)/shard_map/attention_forward/pallas_call | solution.py:90
  147.1 9.0 %fusion.69 = f32[1024,3072]{1,0:T(8,128)} fusion(bf16[768,3072]{1,0:T(8,128)(2,1)S(1)} %bitcast.147, f32[1024,768]{0,1:T(8,128)S(1)} %get-tuple-element.149, f32[768]{0:T(1024)S(1)} %convert_element_type.138, f32[768]{0:T(1024)S(1)} %convert_element_type.137, f32[1024]{0:T(1024)S(1)} %fusion.62, f32[1024]{0:T(1024)S(1)} %broadcast_multiply_fusion), kind=kOutput, calls=%fused_computation.144 | convolution fusion | flops 4835770368 | bytes 20461568 | tf_op jit(solution)/shard_map/dot_general | solution.py:30
  156.1 11.7 %convolution_convert_fusion.1 = bf16[3072,768]{1,0:T(8,128)(2,1)} fusion(bf16[1024,768]{1,0:T(8,128)(2,1)S(1)} %copy-done.14, f32[1024,3072]{1,0:T(8,128)} %fusion.69), kind=kOutput, calls=%fused_computation.16 | convolution fusion | flops 4862509056 | bytes 18874368 | tf_op jit(solution)/shard_map/dot_general | solution.py:30
  167.8 11.2 %add_convert_fusion.1 = bf16[1024,768]{0,1:T(8,128)(2,1)} fusion(f32[1024,768]{0,1:T(8,128)S(1)} %get-tuple-element.149, bf16[3072,768]{1,0:T(8,128)(2,1)} %param.40, f32[1024,3072]{1,0:T(8,128)} %fusion.69), kind=kOutput, calls=%fused_computation.43 | convolution fusion | flops 4861722624 | bytes 22020096 | tf_op jit(solution)/shard_map/dot_general | solution.py:30
  179.0 15.2 %fusion.6 = bf16[1024,3072]{1,0:T(8,128)(2,1)} fusion(f32[1024,3072]{1,0:T(8,128)} %fusion.69, bf16[1024,768]{1,0:T(8,128)(2,1)S(1)} %copy-done.14, bf16[3072,768]{1,0:T(8,128)(2,1)} %param.40), kind=kOutput, calls=%fused_computation.12 | convolution fusion | flops 4894752768 | bytes 25165824 | tf_op jit(solution)/shard_map/dot_general | solution.py:30
  194.3 8.8 %multiply_reduce_fusion.2 = (bf16[768]{0:T(1024)(128)(2,1)S(1)}, f32[1024]{0:T(1024)S(1)}, bf16[768]{0:T(1024)(128)(2,1)S(1)}, f32[1024,768]{0,1:T(8,128)S(1)}) fusion(f32[1024,768]{0,1:T(8,128)S(1)} %get-tuple-element.149, f32[1024]{0:T(1024)S(1)} %fusion.62, f32[1024]{0:T(1024)S(1)} %broadcast_multiply_fusion, f32[768]{0:T(1024)S(1)} %convert_element_type.137, ...), kind=kOutput, calls=%fused_computation.40 | convolution fusion | flops 4838126592 | bytes 17319936 | tf_op jit(solution)/shard_map/dot_general | solution.py:30
  203.1 7.1 %convolution_convert_fusion = bf16[768,3072]{1,0:T(8,128)(2,1)} fusion(bf16[1024,3072]{1,0:T(8,128)(2,1)S(1)} %copy-done.53, f32[1024,768]{0,1:T(8,128)S(1)} %get-tuple-element.149, f32[768]{0:T(1024)S(1)} %convert_element_type.138, f32[768]{0:T(1024)S(1)} %convert_element_type.137, f32[1024]{0:T(1024)S(1)} %fusion.62, f32[1024]{0:T(1024)S(1)} %broadcast_multiply_fusion), kind=kOutput, calls=%fused_computation.15 | convolution fusion | flops 4838129664 | bytes 14170112 | tf_op jit(solution)/shard_map/dot_general | solution.py:30
  215.1 2.6 fusion.42.g_ref
  217.7 9.8 %reshape.288 = bf16[32,24,4,768]{3,2,1,0:T(4,128)(2,1)} reshape(bf16[768,3072]{1,0:T(8,128)(2,1)} %convolution_convert_fusion) | data formatting | bytes 9437184 | tf_op jit(solution)/shard_map/reshape | solution.py:671
  227.5 5.4 %copy.115 = bf16[32,24,4,768]{3,1,2,0:T(8,128)(2,1)} copy(bf16[32,24,4,768]{3,2,1,0:T(4,128)(2,1)} %reshape.288) | data formatting | bytes 9437184 | tf_op jit(solution)/shard_map/reshape | solution.py:671
  233.3 6.7 %pad_maximum_fusion.refs_1_ = bf16[4,2,2,2,128,768]{5,4,3,2,1,0:T(8,128)(2,1)} fusion(bf16[4,2,2,2,8,768]{5,4,3,2,1,0:T(8,128)(2,1)S(1)} %bitcast.149, bf16[4,2,2,2,24,768]{5,4,3,2,1,0:T(8,128)(2,1)} %bitcast.151, bf16[4,2,2,2,96,768]{5,4,3,2,1,0:T(8,128)(2,1)} %bitcast.143), kind=kLoop, calls=%fused_computation.14 | loop fusion | flops 18874368 | bytes 12582912 | tf_op jit(solution)/shard_map/concatenate | solution.py:415
  240.0 83.1 %attention_backward.1 = (bf16[3,768,1024]{2,1,0:T(8,128)(2,1)}, f32[96,768]{1,0:T(8,128)}, f32[128,768]{1,0:T(8,128)}) custom-call(bf16[768,1024]{1,0:T(8,128)(2,1)} %copy-done.3, bf16[768,1024]{1,0:T(8,128)(2,1)} %copy-done.2, bf16[768,1024]{1,0:T(8,128)(2,1)} %copy-done.1, bf16[768,1024]{1,0:T(8,128)(2,1)} %copy-done.4, bf16[768,1024]{1,0:T(8,128)(2,1)} %fusion.42.g_ref, ...), custom_call_target="tpu_custom_call" | custom-call | tf_op jit(solution)/shard_map/attention_backward/pallas_call | solution.py:196
  325.7 4.1 fusion.36
  335.7 4.0 multiply_reduce_fusion.1
  341.6 2.9 fusion.70
  348.9 3.6 fusion.19
  358.0 3.0 convolution_convert_fusion.8
  365.2 91.9 %tail.1 = (f32[4128,192]{1,0:T(8,128)}, f32[80,768]{1,0:T(8,128)}, f32[80,768]{1,0:T(8,128)}) custom-call(bf16[4,192,1024]{2,1,0:T(8,128)(2,1)} %bitcast.145, s32[4,1024,1]{2,1,0:T(8,128)} %broadcast_in_dim.90.slots_ref, s32[8,1,768]{2,1,0:T(1,128)} %reshape.292.ids_ref, bf16[4,2,2,2,80,768]{5,4,3,2,1,0:T(8,128)(2,1)} %pad_maximum_fusion.1.refs_0_, ...), custom_call_target="tpu_custom_call" | custom-call | tf_op jit(solution)/shard_map/tail/pallas_call | solution.py:564
  461.6 3.1 fusion.78
  467.1 5.3 %copy.125 = f32[4128,192]{0,1:T(8,128)} copy(f32[4128,192]{1,0:T(8,128)} %get-tuple-element.105) | data formatting | bytes 6340608
  (198 shorter events, 64.2 us)
Async XLA Ops:
  0.7 56.8 %copy-start = (bf16[1024,768]{1,0:T(8,128)(2,1)S(1)}, bf16[1024,768]{1,0:T(8,128)(2,1)}, u32[]{:S(2)}) copy-start(bf16[1024,768]{1,0:T(8,128)(2,1)} %param.21) | copy-start | bytes 4718596
  35.3 5.1 %copy-start.34 = (bf16[768]{0:T(1024)(128)(2,1)S(1)}, bf16[768]{0:T(1024)(128)(2,1)}, u32[]{:S(2)}) copy-start(bf16[768]{0:T(1024)(128)(2,1)} %param.31) | copy-start | bytes 4612
  35.3 5.1 %copy-start.35 = (bf16[768]{0:T(1024)(128)(2,1)S(1)}, bf16[768]{0:T(1024)(128)(2,1)}, u32[]{:S(2)}) copy-start(bf16[768]{0:T(1024)(128)(2,1)} %param.37) | copy-start | bytes 4612
  35.3 5.2 %copy-start.36 = (bf16[768]{0:T(1024)(128)(2,1)S(1)}, bf16[768]{0:T(1024)(128)(2,1)}, u32[]{:S(2)}) copy-start(bf16[768]{0:T(1024)(128)(2,1)} %param.38) | copy-start | bytes 4612
  35.3 5.2 %copy-start.37 = (bf16[768]{0:T(1024)(128)(2,1)S(1)}, bf16[768]{0:T(1024)(128)(2,1)}, u32[]{:S(2)}) copy-start(bf16[768]{0:T(1024)(128)(2,1)} %param.32) | copy-start | bytes 4612
  35.3 5.2 %copy-start.13 = (bf16[1024,768]{1,0:T(8,128)(2,1)S(1)}, bf16[1024,768]{1,0:T(8,128)(2,1)}, u32[]{:S(2)}) copy-start(bf16[1024,768]{1,0:T(8,128)(2,1)} %param.41) | copy-start | bytes 4718596
  35.3 42.8 %all-to-all-start.1 = ((bf16[8,192,768]{2,1,0:T(8,128)(2,1)}), bf16[8,192,768]{2,1,0:T(8,128)(2,1)}, u32[]{:S(2)}, u32[]{:S(2)}) async-start(bf16[8,192,768]{2,1,0:T(8,128)(2,1)} %broadcast_select_fusion), calls=%async_computation.1 | async-start | bytes 4718592 | tf_op jit(solution)/shard_map/all_to_all | solution.py:632
  40.4 51.3 %copy-start.26 = (f32[768]{0:T(1024)}, f32[768]{0:T(1024)S(1)}, u32[]{:S(2)}) copy-start(f32[768]{0:T(1024)S(1)} %convert_element_type.128) | copy-start | bytes 9220
  57.4 4.5 copy-start.47
  63.4 3.3 copy-start.50
  91.2 53.0 %copy-start.6 = (f32[1024,768]{0,1:T(8,128)}, f32[1024,768]{0,1:T(8,128)S(1)}, u32[]{:S(2)}) copy-start(f32[1024,768]{0,1:T(8,128)S(1)} %get-tuple-element.147) | copy-start | bytes 9437188
  91.7 3.4 copy-start.30
  91.7 3.4 copy-start.28
  93.6 3.3 copy-start.16
  95.5 3.3 copy-start.1
  98.8 45.4 %copy-start.3 = (bf16[768,1024]{1,0:T(8,128)(2,1)}, bf16[768,1024]{1,0:T(8,128)(2,1)S(1)}, u32[]{:S(2)}) copy-start(bf16[768,1024]{1,0:T(8,128)(2,1)S(1)} %fusion.39.q_ref) | copy-start | bytes 4718596
  98.8 45.4 %copy-start.38 = (bf16[768,768]{1,0:T(8,128)(2,1)S(1)}, bf16[768,768]{1,0:T(8,128)(2,1)}, u32[]{:S(2)}) copy-start(bf16[768,768]{1,0:T(8,128)(2,1)} %param.36) | copy-start | bytes 3538948
  144.2 68.1 %copy-start.4 = (bf16[768,1024]{1,0:T(8,128)(2,1)}, bf16[768,1024]{1,0:T(8,128)(2,1)S(1)}, u32[]{:S(2)}) copy-start(bf16[768,1024]{1,0:T(8,128)(2,1)S(1)} %get-tuple-element.26.o_ref) | copy-start | bytes 4718596
  147.1 9.0 %copy-start.14 = (bf16[1024,768]{1,0:T(8,128)(2,1)S(1)}, bf16[1024,768]{1,0:T(8,128)(2,1)}, u32[]{:S(2)}) copy-start(bf16[1024,768]{1,0:T(8,128)(2,1)} %param.41) | copy-start | bytes 4718596
  194.3 8.9 %copy-start.53 = (bf16[1024,3072]{1,0:T(8,128)(2,1)S(1)}, bf16[1024,3072]{1,0:T(8,128)(2,1)}, u32[]{:S(2)}) copy-start(bf16[1024,3072]{1,0:T(8,128)(2,1)} %fusion.6) | copy-start | bytes 18874372
  240.0 85.7 %copy-start.17 = (bf16[1024,768]{0,1:T(8,128)(2,1)S(1)}, bf16[1024,768]{0,1:T(8,128)(2,1)}, u32[]{:S(2)}) copy-start(bf16[1024,768]{0,1:T(8,128)(2,1)} %copy-done.16) | copy-start | bytes 4718596
  324.6 5.3 %slice-start.2 = ((s8[4718592]{0:T(1024)(128)(4,1)}), s8[4194304]{0:T(1024)(128)(4,1)S(1)}, s32[]{:S(2)}) async-start(s8[4718592]{0:T(1024)(128)(4,1)} %bitcast.168), calls=%async_computation.4 | async-start | bytes 8388608
  325.7 4.1 slice-start.3
  332.3 3.4 copy-start.44
  335.7 4.0 copy-start.31
  335.7 4.0 copy-start.29
  348.9 3.6 copy-start.12
  358.0 3.0 copy-start.18
  365.2 96.5 %copy-start.49 = (bf16[768,768]{1,0:T(8,128)(2,1)S(1)}, bf16[768,768]{1,0:T(8,128)(2,1)}, u32[]{:S(2)}) copy-start(bf16[768,768]{1,0:T(8,128)(2,1)} %param.28) | copy-start | bytes 3538948
  365.2 96.5 %copy-start.52 = (bf16[1024,768]{0,1:T(8,128)(2,1)S(1)}, bf16[1024,768]{0,1:T(8,128)(2,1)}, u32[]{:S(2)}) copy-start(bf16[1024,768]{0,1:T(8,128)(2,1)} %add_convert_fusion) | copy-start | bytes 4718596
  461.6 3.1 copy-start.15
  467.1 5.3 %copy-start.23 = (f32[96,768]{1,0:T(8,128)S(1)}, f32[96,768]{1,0:T(8,128)}, u32[]{:S(2)}) copy-start(f32[96,768]{1,0:T(8,128)} %get-tuple-element.191) | copy-start | bytes 884740
  (27 other events, 57.0 us)

commit v3 on v2

--- a/solution.py
+++ b/solution.py
@@ -487,7 +487,7 @@
 
     def sort(self, step):
         owner = lax.rem(self.emb + step, self.owners)
-        lanes = lax.broadcasted_iota(jnp.int32, (self.length, 128), 1)
+        rows = lax.broadcasted_iota(jnp.int32, (128, self.length), 0)
         tiles = []
         for tile in range(self.wide // 128):
             total = jnp.zeros((self.columns, 128), jnp.float32)
@@ -495,12 +495,11 @@
                 low, high = group * self.capacity, (group + 1) * self.capacity
                 if high <= tile * 128 or low >= (tile + 1) * 128:
                     continue
-                source = lax.rem(self.group - group + self.groups, self.groups)
-                slot = lanes + (tile * 128 - low)
+                slot = rows + (tile * 128 - low)
                 inside = (slot >= 0) & (slot < self.capacity)
                 wanted = jnp.where(inside, slot + owner * self.capacity, -2)
-                hot = jnp.where(wanted == self.slots[source], 1.0, 0.0).astype(jnp.bfloat16)
-                total = total + product(self.turned[group], hot)
+                hot = jnp.where(wanted == self.slots[group], 1.0, 0.0).astype(jnp.bfloat16)
+                total = total + product_right(self.turned[group], hot)
             tiles.append(total.astype(jnp.bfloat16))
         self.packed[owner] = jnp.concatenate(tiles, 1)
         return owner
@@ -573,6 +572,255 @@
         ),
         name="tail",
     )(grads, slots, ids, *packs)
+
+
+def column_of(row, rows):
+    diagonal = lax.broadcasted_iota(jnp.int32, (128, 128), 0) == lax.broadcasted_iota(
+        jnp.int32, (128, 128), 1
+    )
+    pieces = [
+        jnp.sum(jnp.where(diagonal, row[:, start : start + 128], 0), 1, keepdims=True)
+        for start in range(0, rows, 128)
+    ]
+    return jnp.concatenate(pieces, 0)
+
+
+def gelu_pair(value):
+    root = 0.7978845608028654
+    square = value * value
+    bend = jnp.tanh(root * (value + 0.044715 * (value * square)))
+    half = 0.5 * (1.0 + bend)
+    slope = half + 0.5 * value * (1.0 - bend * bend) * (root * (1.0 + 3 * 0.044715 * square))
+    return value * half, slope
+
+
+def front_kernel(
+    counts_ref,
+    codes_ref,
+    place_ref,
+    pixels_ref,
+    table_ref,
+    pos_ref,
+    w_patch_ref,
+    w_a_ref,
+    w_b_ref,
+    gain_ref,
+    bias_ref,
+    embedded_ref,
+    normed_ref,
+    first_ref,
+    act_ref,
+    slope_ref,
+    ids_ref,
+    slots_ref,
+    codes_all,
+    ranks,
+    earlier,
+    held,
+    packed,
+    landed,
+    fetched,
+    mixed,
+    local_sem,
+    ask_send,
+    ask_got,
+    send,
+    got,
+):
+    owners, capacity, width = packed.shape
+    length = codes_ref.shape[1]
+    table_rows = held.shape[0]
+    emb = lax.axis_index("emb")
+    bring = pltpu.make_async_copy(table_ref, held, local_sem.at[0])
+    bring.start()
+    barrier = pltpu.get_barrier_semaphore()
+    for step in range(1, owners):
+        other = lax.rem(emb + step, owners)
+        pl.semaphore_signal(barrier, inc=1, device_id={"emb": other}, device_id_type=MESH)
+    pl.semaphore_wait(barrier, owners - 1)
+
+    def ask(step):
+        return pltpu.make_async_remote_copy(
+            src_ref=codes_ref,
+            dst_ref=codes_all.at[step],
+            send_sem=ask_send.at[step - 1],
+            recv_sem=ask_got.at[step - 1],
+            device_id={"emb": lax.rem(emb + step, owners)},
+            device_id_type=MESH,
+        )
+
+    def give(step):
+        return pltpu.make_async_remote_copy(
+            src_ref=packed.at[step],
+            dst_ref=landed.at[step - 1],
+            send_sem=send.at[step - 1],
+            recv_sem=got.at[step - 1],
+            device_id={"emb": lax.rem(emb - step + owners, owners)},
+            device_id_type=MESH,
+        )
+
+    for step in range(1, owners):
+        ask(step).start()
+    codes_all[0] = codes_ref[...]
+    block = min(256, length)
+
+    def triangle(number, carry):
+        base = pl.multiple_of(number * block, block)
+        above = base + lax.broadcasted_iota(jnp.int32, (block, length), 0)
+        below = lax.broadcasted_iota(jnp.int32, (block, length), 1)
+        earlier[pl.ds(base, block), :] = jnp.where(above < below, 1.0, 0.0).astype(jnp.bfloat16)
+        return carry
+
+    lax.fori_loop(0, length // block, triangle, 0)
+    codes = codes_ref[...]
+    mine = [
+        (codes >= owner * table_rows) & (codes < (owner + 1) * table_rows)
+        for owner in range(owners)
+    ]
+    marks = jnp.concatenate([jnp.where(mark, 1.0, 0.0) for mark in mine], 0)
+    places = product(marks.astype(jnp.bfloat16), earlier[...])
+    slots = jnp.full((1, length), owners * capacity, jnp.int32)
+    for owner in range(owners):
+        rank = places[owner : owner + 1].astype(jnp.int32)
+        slots = jnp.where(mine[owner], owner * capacity + rank, slots)
+    slots_ref[...] = slots
+    for step in range(1, owners):
+        ask(step).wait()
+    local = codes_all[...].reshape(owners, length) - emb * table_rows
+    inside = (local >= 0) & (local < table_rows)
+    places = product(jnp.where(inside, 1.0, 0.0).astype(jnp.bfloat16), earlier[...])
+    ranks[...] = jnp.where(inside, places.astype(jnp.int32), -1).reshape(owners, 1, length)
+    bring.wait()
+
+    def gather(step):
+        rank = ranks[step]
+        local = codes_all[step] - emb * table_rows + 1
+        slot = lax.broadcasted_iota(jnp.int32, (capacity, length), 0)
+        match = slot == rank
+        hot = jnp.where(match, 1.0, 0.0).astype(jnp.bfloat16)
+        coarse = lax.div(local, 64)
+        fine = local - coarse * 64
+        inner = rank >= 0
+        pair = jnp.concatenate(
+            [jnp.where(inner, coarse, 0), jnp.where(inner, fine, 0)]
+            + [jnp.zeros((6, length), jnp.int32)],
+            0,
+        )
+        pair = product_right(pair.astype(jnp.float32).astype(jnp.bfloat16), hot)
+        source = lax.rem(emb - step + owners, owners)
+        ids_ref[source] = (pair[0:1] * 64.0 + pair[1:2]).astype(jnp.int32) - 1
+        wanted = jnp.sum(jnp.where(match, local, 0), 1, keepdims=True) - 1
+        total = jnp.zeros((capacity, width), jnp.float32)
+        for start in range(0, table_rows, 1024):
+            size = min(1024, table_rows - start)
+            row = start + lax.broadcasted_iota(jnp.int32, (capacity, size), 1)
+            hot = jnp.where(row == wanted, 1.0, 0.0).astype(jnp.bfloat16)
+            total = total + product(hot, held[start : start + size, :])
+        packed[step] = total.astype(jnp.bfloat16)
+
+    def serve(step, carry):
+        gather(step)
+        give(step).start()
+        return carry
+
+    lax.fori_loop(1, owners, serve, 0)
+    gather(0)
+    slot_column = column_of(slots, length)
+    fetched[...] = jnp.zeros_like(fetched)
+
+    def place_rows(step):
+        owner = lax.rem(emb + step, owners)
+        rows = packed[0] if step == 0 else landed[step - 1]
+        for start in range(0, length, block):
+            slot = owner * capacity + lax.broadcasted_iota(jnp.int32, (block, capacity), 1)
+            hot = jnp.where(slot == slot_column[start : start + block], 1.0, 0.0)
+            fetched[start : start + block, :] += product(hot.astype(jnp.bfloat16), rows)
+
+
+    def patches(number, carry):
+        base = pl.multiple_of(number * block, block)
+        rows = pl.ds(base, block)
+        first = product(pixels_ref[rows, :], w_patch_ref[...])
+        low = first.astype(jnp.bfloat16)
+        first_ref[rows, :] = low
+        act, slope = gelu_pair(product(low, w_a_ref[...]))
+        act = act.astype(jnp.bfloat16)
+        act_ref[rows, :] = act
+        slope_ref[rows, :] = slope.astype(jnp.bfloat16)
+        mixed[rows, :] = first + product(act, w_b_ref[...])
+        return carry
+
+    lax.fori_loop(0, length // block, patches, 0)
+
+    def positions(number, carry):
+        base = pl.multiple_of(number * block, block)
+        spot = lax.broadcasted_iota(jnp.int32, (block, pos_ref.shape[0]), 1)
+        place = column_of(place_ref[:, pl.ds(base, block)], block)
+        hot = jnp.where(spot == place, 1.0, 0.0).astype(jnp.bfloat16)
+        embedded_ref[pl.ds(base, block), :] = product(hot, pos_ref[...])
+        return carry
+
+    lax.fori_loop(0, length // block, positions, 0)
+    place_rows(0)
+    for step in range(1, owners):
+        give(step).wait()
+        place_rows(step)
+
+    def settle(number, carry):
+        base = pl.multiple_of(number * block, block)
+        rows = pl.ds(base, block)
+        token = base + lax.broadcasted_iota(jnp.int32, (block, width), 0)
+        image = mixed[rows, :] + embedded_ref[rows, :]
+        value = jnp.where(token < counts_ref[0, 0], image, fetched[rows, :])
+        embedded_ref[rows, :] = value
+        normed = normalize(value) * gain_ref[...] + bias_ref[...]
+        normed_ref[rows, :] = normed.astype(jnp.bfloat16)
+        return carry
+
+    lax.fori_loop(0, length // block, settle, 0)
+
+
+def front(counts, codes, place, pixels, table, pos, w_patch, w_a, w_b, gain, bias, capacity):
+    owners = lax.axis_size("emb")
+    length, width = pixels.shape
+    vmem = pl.BlockSpec(memory_space=pltpu.VMEM)
+    low = jax.ShapeDtypeStruct((length, width), jnp.bfloat16)
+    full = jax.ShapeDtypeStruct((length, width), jnp.float32)
+    return pl.pallas_call(
+        front_kernel,
+        in_specs=[pl.BlockSpec(memory_space=pltpu.SMEM), vmem, vmem, vmem]
+        + [pl.BlockSpec(memory_space=pl.ANY)]
+        + [vmem] * 6,
+        out_specs=[vmem] * 7,
+        out_shape=[
+            full,
+            low,
+            low,
+            low,
+            low,
+            jax.ShapeDtypeStruct((owners, 1, capacity), jnp.int32),
+            jax.ShapeDtypeStruct((1, length), jnp.int32),
+        ],
+        scratch_shapes=[
+            pltpu.VMEM((owners, 1, length), jnp.int32),
+            pltpu.VMEM((owners, 1, length), jnp.int32),
+            pltpu.VMEM((length, length), jnp.bfloat16),
+            pltpu.VMEM(table.shape, jnp.bfloat16),
+            pltpu.VMEM((owners, capacity, width), jnp.bfloat16),
+            pltpu.VMEM((owners - 1, capacity, width), jnp.bfloat16),
+            pltpu.VMEM((length, width), jnp.float32),
+            pltpu.VMEM((length, width), jnp.float32),
+            pltpu.SemaphoreType.DMA((1,)),
+            pltpu.SemaphoreType.DMA((owners - 1,)),
+            pltpu.SemaphoreType.DMA((owners - 1,)),
+            pltpu.SemaphoreType.DMA((owners - 1,)),
+            pltpu.SemaphoreType.DMA((owners - 1,)),
+        ],
+        compiler_params=pltpu.CompilerParams(
+            collective_id=1, has_side_effects=True, vmem_limit_bytes=56 << 20
+        ),
+        name="front",
+    )(counts, codes, place, pixels, table, pos, w_patch, w_a, w_b, gain, bias)
 
 
 def on_device(
@@ -608,46 +856,37 @@
     rows_owned = token_table.shape[0]
     owners_total = lax.axis_size("emb")
     capacity = 3 * length // (2 * owners_total)
-    owner_index = row_ids // rows_owned
-    local_row = row_ids - owner_index * rows_owned
-    owner_hot = (
-        (owner_index[:, None] == jnp.arange(owners_total)[None, :]) & table_rows[:, None]
-    ).astype(jnp.int32)
-    earlier = jnp.cumsum(owner_hot, 0) - owner_hot
-    rank_within = jnp.sum(earlier * owner_hot, 1)
-    slot_index = jnp.where(
-        table_rows, owner_index * capacity + rank_within, owners_total * capacity
+    groups = lax.axis_size("dp")
+    codes = jnp.where(table_rows, row_ids, -1).reshape(1, length)
+    gain_row = gain_one.astype(jnp.float32).reshape(1, model_width)
+    bias_row = bias_one.astype(jnp.float32).reshape(1, model_width)
+    embedded, normed_one, first_low, res_act, res_slope, ids, slots = front(
+        counts,
+        codes,
+        patch_pos.reshape(1, length),
+        pixels,
+        token_table,
+        pos_table,
+        w_patch,
+        w_res_a,
+        w_res_b,
+        gain_row,
+        bias_row,
+        capacity,
     )
-    request = (
-        jnp.full((owners_total * capacity + 1,), -1, jnp.int32)
-        .at[slot_index]
-        .set(jnp.where(table_rows, local_row, -1))
-    )
-    received = lax.all_to_all(
-        request[:-1].reshape(owners_total, capacity), "emb", split_axis=0, concat_axis=0, tiled=True
-    )
-    valid_slots = received >= 0
-    local_ids = jnp.maximum(received, 0)
-    fetched = jnp.where(valid_slots[..., None], token_table[local_ids], jnp.zeros((), jnp.bfloat16))
-    returned = lax.all_to_all(fetched, "emb", split_axis=0, concat_axis=0, tiled=True)
-    slot_safe = jnp.minimum(slot_index, owners_total * capacity - 1)
-    table_embed = returned.reshape(owners_total * capacity, model_width)[slot_safe].astype(
-        jnp.float32
-    )
-    patch_first = product(pixels, w_patch)
-    first_low = patch_first.astype(jnp.bfloat16)
-    res_inner = product(first_low, w_res_a)
-    res_gelu, gelu_back_res = jax.vjp(jax.nn.gelu, res_inner)
-    res_act = res_gelu.astype(jnp.bfloat16)
-    res_mixed = product(res_act, w_res_b)
     position_hot = patch_pos[:, None] == jnp.arange(pos_table.shape[0])[None, :]
-    position_embed = product(position_hot.astype(jnp.bfloat16), pos_table)
-    image_embed = patch_first + res_mixed + position_embed
-    embedded = jnp.where(image_rows[:, None], image_embed, table_embed)
-    normed_one_f, norm_back_one = jax.vjp(
+    facts = jnp.concatenate([ids.reshape(-1), slots.reshape(-1)])
+    ring = [facts] + [
+        lax.ppermute(facts, "dp", [(i, (i + step) % groups) for i in range(groups)])
+        for step in range(1, groups)
+    ]
+    ring = jnp.stack(ring)
+    ring_ids = ring[:, : owners_total * capacity].reshape(groups, owners_total, capacity)
+    ring_ids = jnp.swapaxes(ring_ids, 0, 1).reshape(owners_total, 1, groups * capacity)
+    ring_slots = ring[:, owners_total * capacity :].reshape(groups, 1, length)
+    _, norm_back_one = jax.vjp(
         norm_affine, embedded, gain_one.astype(jnp.float32), bias_one.astype(jnp.float32)
     )
-    normed_one = normed_one_f.astype(jnp.bfloat16)
     queries = contract(w_q, normed_one, 0, 1).astype(jnp.bfloat16)
     key_heads = contract(w_k, normed_one, 0, 1).astype(jnp.bfloat16)
     value_heads = contract(w_v, normed_one, 0, 1).astype(jnp.bfloat16)
@@ -664,12 +903,13 @@
     grad_w_down = product_left(up_low, cotangent)
     (grad_up_pre,) = gelu_back_up(product_right(cotangent, w_down))
     grad_up = grad_up_pre.astype(jnp.bfloat16)
-    grad_w_up = product_left(normed_two, grad_up).astype(jnp.bfloat16)
     devices = lax.axis_size("dp") * owners_total
     share = model_width // devices
-    folds = grad_w_up.shape[1] // model_width
-    folded = grad_w_up.reshape(devices, share, folds, model_width)
-    folded = jnp.swapaxes(folded, 1, 2).reshape(devices, folds * share, model_width)
+    folds = w_up.shape[1] // model_width
+    folded = [
+        rows_of(product_left(normed_two, grad_up[:, n * model_width : (n + 1) * model_width]))
+        for n in range(folds)
+    ]
     grad_normed_two = product_right(grad_up, w_up)
     grad_middle_norm, grad_gain_two, grad_bias_two = norm_back_two(grad_normed_two)
     grad_middle = cotangent.astype(jnp.float32) + grad_middle_norm
@@ -685,7 +925,7 @@
         grad_attended,
         probs,
         inverse,
-        [stacked([rows_of(grad_w_down)]), stacked([folded, rows_of(grad_w_o), gains_two])],
+        [stacked([rows_of(grad_w_down)]), stacked(folded + [rows_of(grad_w_o), gains_two])],
     )
     grad_heads = grad_heads.reshape(3 * model_width, length)
     grad_normed_one = product_left(grad_heads, jnp.concatenate([w_q.T, w_k.T, w_v.T], 0))
@@ -697,20 +937,14 @@
     ]
     grad_embedded = grad_middle + grad_embed_norm
     grad_low = grad_embedded.astype(jnp.bfloat16)
-    groups = lax.axis_size("dp")
     columns = model_width // groups
-    all_ids = lax.all_gather(received, "dp", axis=0, tiled=False)
-    all_ids = jnp.swapaxes(all_ids, 0, 1)
-    turned = (groups - jnp.arange(groups) + lax.axis_index("dp")) % groups
-    all_ids = all_ids[:, turned].reshape(owners_total, 1, groups * capacity)
-    all_slots = lax.all_gather(slot_index, "dp", axis=0, tiled=False)[:, :, None]
     grads_turned = grad_low.T.reshape(groups, columns, length)
     grad_image = jnp.where(image_rows[:, None], grad_embedded, 0.0)
     grad_mixed = grad_image.astype(jnp.bfloat16)
     grad_pos_table = product_left(position_hot.astype(jnp.bfloat16), grad_mixed)
     grad_w_res_b = product_left(res_act, grad_mixed)
-    (grad_inner_f,) = gelu_back_res(product_right(grad_mixed, w_res_b))
-    grad_inner = grad_inner_f.astype(jnp.bfloat16)
+    grad_inner = product_right(grad_mixed, w_res_b) * res_slope.astype(jnp.float32)
+    grad_inner = grad_inner.astype(jnp.bfloat16)
     grad_w_res_a = product_left(first_low, grad_inner)
     grad_first = (grad_image + product_right(grad_inner, w_res_a)).astype(jnp.bfloat16)
     grad_w_patch = product_left(pixels, grad_first)
@@ -718,8 +952,8 @@
     res_rows = [rows_of(g) for g in (grad_w_patch, grad_w_res_a, grad_w_res_b, grad_pos_table)]
     grad_table, share_heads, share_res = tail(
         grads_turned,
-        all_slots,
-        all_ids,
+        ring_slots,
+        ring_ids,
         [stacked(grad_w_heads + [gains_one]), stacked(res_rows)],
         rows_owned,
         capacity,

time: 482 us -> 456 us (0.946)
  the two profiles are of different devices: /device:TPU:9 before, /device:TPU:1 now
where the time goes in v3:
time: 456 us; the launch traced here: 447 us
  Pallas kernels  260 us (57%)
  matrix products  109 us (24%)
  local copies, waits for them, and re-layouts  44.1 us (10%)
  other arithmetic  28.3 us (6%)
    dot_general x26, matrix products, contract(): lax.dot_general(left, right, (((left_dim,), (right_dim,)), ((), ())), pre...  109 us
    pallas_call x1, Pallas kernels, tail(): pl.pallas_call(functools.partial(tail_kernel, len(packs)), in_specs=[anyw...  89 us
    pallas_call x1, Pallas kernels, attention_backward(): pl.pallas_call(functools.partial(backward_kernel, HEADS_STEP, len(packs))...  78.4 us
    pallas_call x1, Pallas kernels, front(): pl.pallas_call(front_kernel, in_specs=[pl.BlockSpec(memory_space=pltpu.SM...  46.9 us
    pallas_call x1, Pallas kernels, attention_forward(): pl.pallas_call(functools.partial(forward_kernel, HEADS_STEP), grid=(heads...  45.4 us
    unnamed x119, local copies, waits for them, and re-layouts  20.6 us
  transfers between devices with their start and end apart: 3, of which 0 were waited for; matrix products, arithmetic and copies ran while one was open for 34% of the time, Pallas kernels for 28%

profile of v3, /device:TPU:1, one launch (start us, length us, event | category | flops | bytes accessed | tf_op | source)
XLA Modules:
  0.0 447.5 jit_solution(921886752792335785)
XLA Ops:
  7.2 46.9 %front.1 = (f32[1024,768]{1,0:T(8,128)}, bf16[1024,768]{1,0:T(8,128)(2,1)}, bf16[1024,768]{1,0:T(8,128)(2,1)}, bf16[1024,768]{1,0:T(8,128)(2,1)}, bf16[1024,768]...) custom-call(s32[1,2]{1,0:T(1,128)} %counts_ref.1, s32[1,1024]{1,0:T(1,128)} %bitcast.136, ...), custom_call_target="tpu_custom_call" | custom-call | tf_op jit(solution)/shard_map/front/pallas_call | solution.py:789
  56.2 3.3 collective-permute-start.2
  62.3 3.0 fusion.54.v_ref
  68.6 45.4 %attention_forward.1 = (bf16[768,1024]{1,0:T(8,128)(2,1)S(1)}, bf16[24,2560,256]{2,1,0:T(8,128)(2,1)}, f32[24,1,1024]{2,1,0:T(1,128)S(1)}) custom-call(bf16[768,1024]{1,0:T(8,128)(2,1)S(1)} %fusion.52.q_ref, bf16[768,1024]{1,0:T(8,128)(2,1)S(1)} %fusion.53.k_ref, bf16[768,1024]{1,0:T(8,128)(2,1)S(1)} %fusion.54.v_ref), custom_call_target="tpu_custom_call" | custom-call | flops 49999998976 | bytes 31457280 | tf_op jit(solution)/shard_map/attention_forward/pallas_call | solution.py:90
  116.8 7.9 %fusion.68 = f32[1024,3072]{1,0:T(8,128)} fusion(bf16[1024,768]{1,0:T(8,128)(2,1)S(1)} %add_convert_fusion.2, bf16[768,3072]{1,0:T(8,128)(2,1)S(1)} %bitcast.142), kind=kOutput, calls=%fused_computation.116 | convolution fusion | flops 4831838208 | bytes 18874368 | tf_op jit(solution)/shard_map/dot_general | solution.py:30
  124.7 11.4 %add_convert_fusion.1 = bf16[1024,768]{1,0:T(8,128)(2,1)} fusion(f32[1024,768]{1,0:T(8,128)S(1)} %get-tuple-element.106, bf16[3072,768]{1,0:T(8,128)(2,1)S(1)} %bitcast.140, f32[1024,3072]{1,0:T(8,128)} %fusion.68), kind=kOutput, calls=%fused_computation.30 | convolution fusion | flops 4861722624 | bytes 22020096 | tf_op jit(solution)/shard_map/dot_general | solution.py:30
  136.1 11.8 %convolution_convert_fusion = bf16[3072,768]{1,0:T(8,128)(2,1)} fusion(bf16[1024,768]{1,0:T(8,128)(2,1)S(1)} %copy-done.16, f32[1024,3072]{1,0:T(8,128)} %fusion.68), kind=kOutput, calls=%fused_computation.10 | convolution fusion | flops 4862509056 | bytes 18874368 | tf_op jit(solution)/shard_map/dot_general | solution.py:30
  147.9 15.5 %fusion.6 = bf16[1024,3072]{1,0:T(8,128)(2,1)} fusion(f32[1024,3072]{1,0:T(8,128)} %fusion.68, bf16[1024,768]{1,0:T(8,128)(2,1)S(1)} %copy-done.16, bf16[3072,768]{1,0:T(8,128)(2,1)S(1)} %bitcast.140), kind=kOutput, calls=%fused_computation.8 | convolution fusion | flops 4894752768 | bytes 25165824 | tf_op jit(solution)/shard_map/dot_general | solution.py:30
  163.4 4.1 fusion.49
  167.5 2.5 fusion.46
  170.0 2.5 fusion.43
  172.5 2.5 fusion.40
  175.0 6.7 %fusion.66 = (bf16[768]{0:T(1024)(128)(2,1)S(1)}, f32[1024,768]{0,1:T(8,128)}) fusion(bf16[1024,3072]{1,0:T(8,128)(2,1)S(1)} %copy-done.50, bf16[768,3072]{1,0:T(8,128)(2,1)S(1)} %bitcast.142), kind=kOutput, calls=%fused_computation.114 | convolution fusion | flops 4832623616 | bytes 14157312 | tf_op jit(solution)/shard_map/dot_general | solution.py:30
  181.7 3.5 copy.55
  185.3 3.9 multiply_reduce_fusion.3
  194.3 2.4 convolution_convert_fusion.8
  196.7 2.6 fusion.55.g_ref
  204.5 2.7 copy-done.15
  207.2 78.4 %attention_backward.1 = (bf16[3,768,1024]{2,1,0:T(8,128)(2,1)}, f32[96,768]{1,0:T(8,128)}, f32[128,768]{1,0:T(8,128)}) custom-call(bf16[768,1024]{1,0:T(8,128)(2,1)} %copy-done.3, bf16[768,1024]{1,0:T(8,128)(2,1)} %copy-done.2, bf16[768,1024]{1,0:T(8,128)(2,1)} %copy-done.1, bf16[768,1024]{1,0:T(8,128)(2,1)} %copy-done.4, bf16[768,1024]{1,0:T(8,128)(2,1)} %fusion.55.g_ref, ...), custom_call_target="tpu_custom_call" | custom-call | tf_op jit(solution)/shard_map/attention_backward/pallas_call | solution.py:196
  285.6 4.5 %fusion.37 = bf16[768,768]{1,0:T(8,128)(2,1)} fusion(bf16[1024,768]{1,0:T(8,128)(2,1)} %get-tuple-element.34, bf16[3,768,1024]{2,1,0:T(8,128)(2,1)} %get-tuple-element.38), kind=kOutput, calls=%fused_computation.60 | convolution fusion | flops 1208549376 | bytes 4325376 | tf_op jit(solution)/shard_map/dot_general | solution.py:30
  290.1 2.5 fusion.34
  292.6 2.5 fusion.31
  295.1 2.2 reduce_sum.114
  297.3 2.5 multiply_reduce_fusion.2
  299.9 7.8 %fusion.67 = (bf16[768]{0:T(1024)(128)(2,1)S(1)}, f32[1024,768]{0,1:T(8,128)}) fusion(bf16[2304,1024]{1,0:T(8,128)(2,1)} %bitcast.143, bf16[768,768]{0,1:T(8,128)(2,1)S(1)} %bitcast.146, bf16[768,768]{0,1:T(8,128)(2,1)S(1)} %bitcast.145, bf16[768,768]{0,1:T(8,128)(2,1)S(1)} %bitcast.144), kind=kOutput, calls=%fused_computation.115 | convolution fusion | flops 3635281152 | bytes 11404800 | tf_op jit(solution)/shard_map/dot_general | solution.py:30
  307.7 3.6 copy.60
  311.3 3.9 multiply_reduce_fusion
  324.6 2.5 convolution_convert_fusion.7
  327.1 3.1 fusion.69
  330.7 3.5 convolution_convert_fusion.5
  347.7 89.0 %tail.1 = (f32[4128,192]{1,0:T(8,128)}, f32[80,768]{1,0:T(8,128)}, f32[80,768]{1,0:T(8,128)}) custom-call(bf16[4,192,1024]{2,1,0:T(8,128)(2,1)} %bitcast.115, s32[4,1,1024]{2,1,0:T(1,128)} %reshape.223.slots_ref, s32[8,1,768]{2,1,0:T(1,128)} %reshape.225.ids_ref, bf16[4,2,2,2,80,768]{5,4,3,2,1,0:T(8,128)(2,1)} %pad_maximum_fusion.refs_0_, ...), custom_call_target="tpu_custom_call" | custom-call | tf_op jit(solution)/shard_map/tail/pallas_call | solution.py:563
  441.2 5.3 %copy.67 = f32[4128,192]{0,1:T(8,128)} copy(f32[4128,192]{1,0:T(8,128)} %get-tuple-element.68) | data formatting | bytes 6340608
  (187 shorter events, 55.1 us)
Async XLA Ops:
  0.7 113.3 %copy-start = (bf16[768,768]{1,0:T(8,128)(2,1)S(1)}, bf16[768,768]{1,0:T(8,128)(2,1)}, u32[]{:S(2)}) copy-start(bf16[768,768]{1,0:T(8,128)(2,1)} %param.36) | copy-start | bytes 3538948
  7.1 54.5 %copy-start.32 = (bf16[768]{0:T(1024)(128)(2,1)S(1)}, bf16[768]{0:T(1024)(128)(2,1)}, u32[]{:S(2)}) copy-start(bf16[768]{0:T(1024)(128)(2,1)} %param.31) | copy-start | bytes 4612
  7.1 55.1 %copy-start.34 = (bf16[768]{0:T(1024)(128)(2,1)S(1)}, bf16[768]{0:T(1024)(128)(2,1)}, u32[]{:S(2)}) copy-start(bf16[768]{0:T(1024)(128)(2,1)} %param.37) | copy-start | bytes 4612
  7.1 55.1 %copy-start.35 = (bf16[768]{0:T(1024)(128)(2,1)S(1)}, bf16[768]{0:T(1024)(128)(2,1)}, u32[]{:S(2)}) copy-start(bf16[768]{0:T(1024)(128)(2,1)} %param.38) | copy-start | bytes 4612
  7.1 55.1 %copy-start.46 = (bf16[768,768]{1,0:T(8,128)(2,1)S(1)}, bf16[768,768]{1,0:T(8,128)(2,1)}, u32[]{:S(2)}) copy-start(bf16[768,768]{1,0:T(8,128)(2,1)} %param.35) | copy-start | bytes 3538948
  56.2 287.8 %collective-permute-start.2 = (s32[2560]{0:T(1024)}, s32[2560]{0:T(1024)}, u32[]{:S(2)}, u32[]{:S(2)}) collective-permute-start(s32[2560]{0:T(1024)} %pad_add_fusion.4), channel_id=1, source_target_pairs={{0,24},{8,0},{16,8},{24,16},{1,25},{9,1},{17,9},{25,17},{2,26},{10... | collective-permute-start | bytes 30728 | tf_op jit(solution)/shard_map/ppermute | solution.py:880
  59.5 285.2 %collective-permute-start.1 = (s32[2560]{0:T(1024)}, s32[2560]{0:T(1024)}, u32[]{:S(2)}, u32[]{:S(2)}) collective-permute-start(s32[2560]{0:T(1024)} %pad_add_fusion.4), channel_id=1, source_target_pairs={{0,16},{8,24},{16,0},{24,8},{1,17},{9,25},{17,1},{25,9},{2,18},{10... | collective-permute-start | bytes 30728 | tf_op jit(solution)/shard_map/ppermute | solution.py:880
  59.5 285.9 %collective-permute-start = (s32[2560]{0:T(1024)}, s32[2560]{0:T(1024)}, u32[]{:S(2)}, u32[]{:S(2)}) collective-permute-start(s32[2560]{0:T(1024)} %pad_add_fusion.4), channel_id=1, source_target_pairs={{0,8},{8,16},{16,24},{24,0},{1,9},{9,17},{17,25},{25,1},{2,10},{10... | collective-permute-start | bytes 30728 | tf_op jit(solution)/shard_map/ppermute | solution.py:880
  62.2 3.0 copy-start.40
  65.3 3.3 copy-start.1
  67.1 49.6 %slice-start.2 = ((s8[4718592]{0:T(1024)(128)(4,1)}), s8[4194304]{0:T(1024)(128)(4,1)S(1)}, s32[]{:S(2)}) async-start(s8[4718592]{0:T(1024)(128)(4,1)} %bitcast.141), calls=%async_computation.2 | async-start | bytes 8388608
  68.6 45.4 %copy-start.3 = (bf16[768,1024]{1,0:T(8,128)(2,1)}, bf16[768,1024]{1,0:T(8,128)(2,1)S(1)}, u32[]{:S(2)}) copy-start(bf16[768,1024]{1,0:T(8,128)(2,1)S(1)} %fusion.52.q_ref) | copy-start | bytes 4718596
  68.6 45.4 %copy-start.7 = (f32[1024,768]{1,0:T(8,128)S(1)}, f32[1024,768]{1,0:T(8,128)}, u32[]{:S(2)}) copy-start(f32[1024,768]{1,0:T(8,128)} %get-tuple-element.33) | copy-start | bytes 9437188
  68.6 48.1 %slice-start.3 = ((s8[4718592]{0:T(1024)(128)(4,1)}), s8[524288]{0:T(1024)(128)(4,1)S(1)}, s32[]{:S(2)}) async-start(s8[4718592]{0:T(1024)(128)(4,1)} %bitcast.141), calls=%async_computation.3 | async-start | bytes 1048576
  115.6 9.0 %copy-start.9 = (f32[1024,768]{1,0:T(8,128)}, f32[1024,768]{1,0:T(8,128)S(1)}, u32[]{:S(2)}) copy-start(f32[1024,768]{1,0:T(8,128)S(1)} %get-tuple-element.106) | copy-start | bytes 9437188
  116.2 8.5 %slice-start = ((s8[4718592]{0:T(1024)(128)(4,1)}), s8[4194304]{0:T(1024)(128)(4,1)S(1)}, s32[]{:S(2)}) async-start(s8[4718592]{0:T(1024)(128)(4,1)} %bitcast.139), calls=%async_computation | async-start | bytes 8388608
  116.8 7.9 %slice-start.1 = ((s8[4718592]{0:T(1024)(128)(4,1)}), s8[524288]{0:T(1024)(128)(4,1)S(1)}, s32[]{:S(2)}) async-start(s8[4718592]{0:T(1024)(128)(4,1)} %bitcast.139), calls=%async_computation.1 | async-start | bytes 1048576
  124.7 11.4 %copy-start.16 = (bf16[1024,768]{1,0:T(8,128)(2,1)S(1)}, bf16[1024,768]{1,0:T(8,128)(2,1)}, u32[]{:S(2)}) copy-start(bf16[1024,768]{1,0:T(8,128)(2,1)} %param.41) | copy-start | bytes 4718596
  163.4 4.1 copy-start.50
  185.2 4.0 copy-start.10
  185.2 4.7 %copy-start.11 = (f32[1024,768]{1,0:T(8,128)S(1)}, f32[1024,768]{1,0:T(8,128)}, u32[]{:S(2)}) copy-start(f32[1024,768]{1,0:T(8,128)} %copy.55) | copy-start | bytes 9437188
  201.1 3.1 copy-start.20
  201.1 3.1 copy-start.21
  285.6 4.5 %copy-start.37 = (bf16[3,768,1024]{2,1,0:T(8,128)(2,1)S(1)}, bf16[3,768,1024]{2,1,0:T(8,128)(2,1)}, u32[]{:S(2)}) copy-start(bf16[3,768,1024]{2,1,0:T(8,128)(2,1)} %get-tuple-element.38) | copy-start | bytes 14155780
  285.6 4.5 %copy-start.41 = (bf16[1024,768]{1,0:T(8,128)(2,1)S(1)}, bf16[1024,768]{1,0:T(8,128)(2,1)}, u32[]{:S(2)}) copy-start(bf16[1024,768]{1,0:T(8,128)(2,1)} %get-tuple-element.34) | copy-start | bytes 4718596
  295.1 4.8 %copy-start.43 = (bf16[768,768]{1,0:T(8,128)(2,1)S(1)}, bf16[768,768]{1,0:T(8,128)(2,1)}, u32[]{:S(2)}) copy-start(bf16[768,768]{1,0:T(8,128)(2,1)} %param.33) | copy-start | bytes 3538948
  307.7 3.6 copy-start.31
  311.3 4.0 copy-start.8
  311.3 4.7 %copy-start.12 = (f32[1024,768]{1,0:T(8,128)S(1)}, f32[1024,768]{1,0:T(8,128)}, u32[]{:S(2)}) copy-start(f32[1024,768]{1,0:T(8,128)} %copy.60) | copy-start | bytes 9437188
  330.7 3.5 copy-start.38
  330.7 3.5 copy-start.49
  441.2 5.4 %copy-start.30 = (f32[96,768]{1,0:T(8,128)S(1)}, f32[96,768]{1,0:T(8,128)}, u32[]{:S(2)}) copy-start(f32[96,768]{1,0:T(8,128)} %get-tuple-element.149) | copy-start | bytes 884740
  (26 other events, 51.0 us)
